TPU v7x, 512 devices: a whole 4x8x8 slice. The times are simulated.
512 devices in a mesh: ctx: 64 (over y_hi, z, core), ch: 8 (over y_lo, x).
Axes of the slice: x: 4, y: 8 (y_hi: 4, y_lo: 2; y = y_hi * 2 + y_lo), z: 8, core: 2. Of those that a mesh axis runs over, the one named last changes fastest.
Arguments:
- inputs: bfloat16 [16384, 4096], P('ctx', 'ch'), may hold values from -6 to 6
- out_grad: bfloat16 [16384, 4096], P('ctx', 'ch'), may hold values from -6 to 6
- decay_rate: float32 [16, 512], replicated, may hold values from 1.5258789e-05 to 0.05, as said below
- residue: float32 [16, 512], replicated, may hold values from -1.5 to 1.5
- skip_gain: float32 [4096], P('ch'), may hold values from -6 to 6
Outputs:
- input_grad: float32 [16384, 4096], P('ctx', 'ch')
- filter_grad: float32 [16384, 512], P('ctx', 'ch')
Inputs may be any that keep to these rules, and one draw needn't show every extreme that they name: `decay_rate`: each decay rate lies either between 0.3 / 16384 and 2 / 16384 or between 1 / 50 and 1 / 25.
All inputs are finite; a program needn't handle non-finite values.
Results may differ from a plain program's by a relative error of at most 0.00055.
Values may be sent and summed in bfloat16 or wider, within the bound.
A program may use at most 64 MiB of HBM per device.

v0:
```python
import functools
import math

import jax
import jax.numpy as jnp
import ml_dtypes
import numpy as np
from jax import lax
from jax.experimental import pallas as pl
from jax.experimental.pallas import tpu as pltpu
from jax.sharding import PartitionSpec as P

MESH = pl.DeviceIdType.MESH
F32 = jnp.float32
BF16 = jnp.bfloat16


def halves(table):
    high = table.astype(np.float32).astype(ml_dtypes.bfloat16)
    low = (table - high.astype(np.float64)).astype(np.float32).astype(ml_dtypes.bfloat16)
    return high, low


@functools.lru_cache(maxsize=None)
def tables(nc, nh, sd):
    rows = 2 * nh
    j = np.arange(nc) + 0.5
    a = np.arange(nc)
    s = np.arange(sd)
    full = 2 * nc * sd
    angle = 2.0 * np.pi * np.outer(j, a) / (2 * nc)
    block = np.concatenate([np.cos(angle), -np.sin(angle)], axis=0)
    high, low = halves(block)
    first = np.concatenate([high, low], axis=1)
    last_h, last_l = halves(block.T.copy())
    last = np.concatenate([last_h, last_h, last_l], axis=1)
    angle = 2.0 * np.pi * np.outer(j, s) / full
    twist = np.stack([np.cos(angle), np.sin(angle)]).astype(np.float32)
    angle = 2.0 * np.pi * (np.outer(s, s) % sd) / sd
    cos, sin = np.cos(angle), np.sin(angle)
    step = np.concatenate([np.concatenate([cos, -sin], axis=1), np.concatenate([sin, cos], axis=1)], axis=0)
    high, low = halves(step)
    second = np.concatenate([high, high, low], axis=0)
    angle = 2.0 * np.pi * np.outer(s + 0.5, s) / (2 * sd)
    near = np.concatenate([np.cos(angle), -np.sin(angle)], axis=0)
    high, low = halves(near)
    near_in = np.concatenate([high, low, high], axis=1)
    near_out = np.concatenate([high.T, high.T, low.T], axis=1)
    size = 16 * rows
    perm = np.zeros((size, size), np.float32)
    for f in range(16):
        for r in range(rows):
            perm[f * rows + r, r * 16 + f] = 1.0
    bf = ml_dtypes.bfloat16
    return (
        perm.astype(bf),
        perm.T.copy().astype(bf),
        first,
        np.ascontiguousarray(second),
        last,
        twist,
        near_in,
        np.ascontiguousarray(near_out),
    )


def split(value):
    high = value.astype(BF16)
    return high, (value - high.astype(F32)).astype(BF16)


def dot(left, right):
    return jnp.dot(left, right, preferred_element_type=F32)


def kernel(nc, nh, modes, *refs):
    (x_ref, g_ref, rate_ref, res_ref, gain_ref), refs = refs[:5], refs[5:]
    table_in, refs = refs[:8], refs[8:]
    (y_ref, out_ref), refs = refs[:2], refs[2:]
    (perm, perm_t, first, second, last, twist, near_in, near_out), refs = refs[:8], refs[8:]
    (s1, r1, s2, r2, u_own, u_all, st_own, st_all, t_own, t_all), refs = refs[:10], refs[10:]
    (grad, taps, eb, ww, rate_rows, blocks, left, spec), refs = refs[:8], refs[8:]
    (table_sem, send1, recv1, send2, recv2, send_u, recv_u, send_s, recv_s, send_t, recv_t) = refs

    sd, cols = x_ref.shape
    rows = 2 * nh
    cb = modes * cols // nc
    nblk = cols // cb
    tiles = sd // 8
    me = lax.axis_index("ctx")
    my = lax.axis_index("ch")

    def ctx_peer(k):
        return lax.rem(me + k, nc)

    def ch_peer(k):
        return lax.rem(my + k, nh)

    barrier = pltpu.get_barrier_semaphore()

    def greet_ch(k, _):
        pl.semaphore_signal(barrier, inc=1, device_id={"ch": ch_peer(k)}, device_id_type=MESH)
        return 0

    def greet_ctx(k, _):
        pl.semaphore_signal(barrier, inc=1, device_id={"ctx": ctx_peer(k)}, device_id_type=MESH)
        return 0

    lax.fori_loop(1, nh, greet_ch, 0)
    lax.fori_loop(1, nc, greet_ctx, 0)

    loads = [
        pltpu.make_async_copy(src, dst, table_sem.at[n])
        for n, (src, dst) in enumerate(
            zip(table_in, (perm, perm_t, first, second, last, twist, near_in, near_out))
        )
    ]
    for load in loads:
        load.start()

    width = min(cols, 256)
    eye = (
        lax.broadcasted_iota(jnp.int32, (width, width), 0)
        == lax.broadcasted_iota(jnp.int32, (width, width), 1)
    ).astype(F32).astype(BF16)
    for arr, ref in enumerate((x_ref, g_ref)):
        for c0 in range(0, cols, width):
            turned = lax.dot_general(
                eye, ref[:, c0 : c0 + width], (((1,), (1,)), ((), ())), preferred_element_type=F32
            ).astype(BF16)
            turned = turned.reshape(width // nc, nc, sd)
            for k in range(width // nc):
                s1[c0 // nc + k, arr] = turned[k]

    pl.semaphore_wait(barrier, nh - 1 + nc - 1)

    def copy1(k, src, dst):
        return pltpu.make_async_remote_copy(
            src_ref=src, dst_ref=dst, send_sem=send1, recv_sem=recv1, device_id={"ch": ch_peer(k)}, device_id_type=MESH
        )

    def send_ch(k, _):
        copy1(k, s1.at[ch_peer(k)], r1.at[my]).start()
        return 0

    lax.fori_loop(1, nh, send_ch, 0)
    r1[pl.ds(my, 1)] = s1[pl.ds(my, 1)]

    grad[...] = g_ref[...].astype(F32)
    eight = lax.broadcasted_iota(jnp.int32, (8, cb), 0).astype(F32)
    octs = 8.0 * lax.broadcasted_iota(jnp.int32, (tiles, cb), 0).astype(F32)

    def weight_of(rate, residue):
        x = 2.0 * rate
        series = 1.0 - x * (1.0 / 7.0)
        for n in (6, 5, 4, 3, 2):
            series = 1.0 - (x * (1.0 / n)) * series
        return residue * jnp.sqrt(x * series)

    def columns(blk):
        return pl.ds(pl.multiple_of(blk * cb, cb), cb)

    def states(blk, _):
        at = columns(blk)
        rate = rate_ref[:, at]
        weight = weight_of(rate, res_ref[:, at])
        ww[:, at] = weight
        for n in range(modes):
            slow = jnp.exp(-rate[n : n + 1] * octs)
            eb[n] = slow
        fine = [jnp.exp(-rate[n : n + 1] * eight) for n in range(modes)]
        scaled = [fine[n] * weight[n : n + 1] for n in range(modes)]
        sums = [jnp.zeros((8, cb), F32) for _ in range(modes)]
        for t in range(tiles):
            g = grad[8 * t : 8 * t + 8, at]
            tap = jnp.zeros((8, cb), F32)
            for n in range(modes):
                level = jnp.broadcast_to(eb[n, t : t + 1], (8, cb))
                sums[n] = sums[n] + level * g
                tap = tap + level * scaled[n]
            taps[8 * t : 8 * t + 8, at] = tap
        for n in range(modes):
            rate_rows[n * nblk + blk] = rate[n : n + 1]
            u_own[n * nblk + blk] = jnp.sum(sums[n] * fine[n], axis=0, keepdims=True)
        return 0

    lax.fori_loop(0, nblk, states, 0)

    def ctx_copy(k, src, dst, send, recv):
        return pltpu.make_async_remote_copy(
            src_ref=src, dst_ref=dst, send_sem=send, recv_sem=recv, device_id={"ctx": ctx_peer(k)}, device_id_type=MESH
        )

    def send_to_ctx(own, everyone, send, recv):
        def body(k, _):
            ctx_copy(k, own.at[ctx_peer(k)], everyone.at[me], send, recv).start()
            return 0

        lax.fori_loop(1, nc, body, 0)
        everyone[pl.ds(me, 1)] = own[pl.ds(me, 1)]

    def wait_ctx(own, everyone, send, recv):
        return ctx_copy(1, own.at[pl.ds(0, nc - 1)], everyone.at[pl.ds(0, nc - 1)], send, recv)

    send_to_ctx(u_own, u_all, send_u, recv_u)

    whole1 = copy1(1, s1.at[pl.ds(0, nh - 1)], r1.at[pl.ds(0, nh - 1)])
    whole1.wait_recv()
    loads[0].wait()
    loads[1].wait()
    for f0 in range(0, nc, 16):
        block = r1[:, :, f0 : f0 + 16, :].reshape(rows * 16, sd)
        s2[f0 : f0 + 16] = dot(perm[...], block).astype(BF16).reshape(16, rows, sd)
    send_to_ctx(s2, r2, send2, recv2)

    wait_ctx(u_own, u_all, send_u, recv_u).wait_recv()
    decay = jnp.exp(-rate_rows[me] * float(sd))
    state = jnp.zeros((1, cb), F32)
    for p in range(nc - 1, -1, -1):
        st_own[p] = state
        state = u_all[p] + decay * state
    send_to_ctx(st_own, st_all, send_s, recv_s)

    loads[6].wait()
    loads[7].wait()
    wide = min(cols, 256)

    def inside(blk, _):
        at = pl.ds(pl.multiple_of(blk * wide, wide), wide)
        g = g_ref[:, at]
        g_spec = dot(near_in[:, : 2 * sd], jnp.concatenate([g, g], axis=0))
        high, low = split(taps[:, at])
        h_spec = dot(near_in[...], jnp.concatenate([high, high, low], axis=0))
        g_re, g_im = g_spec[:sd], g_spec[sd:]
        h_re, h_im = h_spec[:sd], h_spec[sd:]
        term = jnp.concatenate([h_re * g_re + h_im * g_im, h_re * g_im - h_im * g_re], axis=0)
        high, low = split(term)
        near = dot(near_out[...], jnp.concatenate([high, low, high], axis=0)) * (1.0 / sd)
        y_ref[:, at] = near + gain_ref[:, at] * grad[:, at]
        return 0

    lax.fori_loop(0, cols // wide, inside, 0)

    wait_ctx(st_own, st_all, send_s, recv_s).wait_recv()

    def outside(blk, _):
        at = columns(blk)
        rate = rate_ref[:, at]
        weight = ww[:, at]
        fine = []
        for n in range(modes):
            carried = weight[n : n + 1] * st_all[n * nblk + blk]
            eb[n] = carried * jnp.exp(-rate[n : n + 1] * (float(sd - 8) - octs))
            fine.append(jnp.exp(-rate[n : n + 1] * (8.0 - eight)))
        for t in range(tiles):
            total = y_ref[8 * t : 8 * t + 8, at]
            for n in range(modes):
                total = total + jnp.broadcast_to(eb[n, t : t + 1], (8, cb)) * fine[n]
            y_ref[8 * t : 8 * t + 8, at] = total
        return 0

    lax.fori_loop(0, nblk, outside, 0)

    for n in (2, 3, 4, 5):
        loads[n].wait()
    wait_ctx(s2, r2, send2, recv2).wait_recv()
    for a0 in range(0, nc, 16):
        block = r2[a0 : a0 + 16].reshape(16 * rows, sd)
        blocks[:, a0 : a0 + 16, :] = dot(perm_t[...], block).astype(BF16).reshape(rows, 16, sd)
    turn_c, turn_s = twist[0], twist[1]
    spec[...] = jnp.zeros_like(spec)

    def pair(q, _):
        for k in range(4):
            part = blocks[4 * q + k]
            freq = dot(first[...], jnp.concatenate([part, part], axis=0))
            re, im = freq[:nc], freq[nc:]
            high_re, low_re = split(re * turn_c + im * turn_s)
            high_im, low_im = split(im * turn_c - re * turn_s)
            at = pl.ds(((k % 2) * 2 + k // 2) * nc, nc)
            for n, piece in enumerate((high_re, high_im, low_re, low_im, high_re, high_im)):
                left[at, n * sd : (n + 1) * sd] = piece
        both = dot(left[...], second[...])
        x_re, x_im = both[: 2 * nc, :sd], both[: 2 * nc, sd:]
        g_re, g_im = both[2 * nc :, :sd], both[2 * nc :, sd:]
        re = x_re * g_re + x_im * g_im
        im = x_re * g_im - x_im * g_re
        spec[:, :sd] += re[:nc] + re[nc:]
        spec[:, sd:] += im[:nc] + im[nc:]
        return 0

    lax.fori_loop(0, nh // 2, pair, 0)

    re_h, re_l = split(spec[:, :sd])
    im_h, im_l = split(-spec[:, sd:])
    both = dot(jnp.concatenate([re_h, im_h, re_l, im_l, re_h, im_h], axis=1), second[...])
    re, im = both[:, :sd], -both[:, sd:]
    high, low = split(
        jnp.concatenate([re * turn_c - im * turn_s, im * turn_c + re * turn_s], axis=0)
    )
    scale = 2.0 / (2 * nc * sd) / math.sqrt(nc * sd * nh)
    result = dot(last[...], jnp.concatenate([high, low, high], axis=0)) * scale
    for d in range(nc):
        t_own[d] = result[d : d + 1]
    send_to_ctx(t_own, t_all, send_t, recv_t)
    wait_ctx(t_own, t_all, send_t, recv_t).wait_recv()
    gathered = jnp.concatenate([t_all[d] for d in range(nc)], axis=0)
    out_ref[...] = gathered.T

    whole1.wait_send()
    wait_ctx(s2, r2, send2, recv2).wait_send()
    wait_ctx(u_own, u_all, send_u, recv_u).wait_send()
    wait_ctx(st_own, st_all, send_s, recv_s).wait_send()
    wait_ctx(t_own, t_all, send_t, recv_t).wait_send()


def body(nc, nh, inputs, out_grad, decay_rate, residue, skip_gain):
    sd, cols = inputs.shape
    modes = decay_rate.shape[0]
    rows = 2 * nh
    cb = modes * cols // nc
    consts = [jnp.asarray(t) for t in tables(nc, nh, sd)]
    vmem = pl.BlockSpec(memory_space=pltpu.VMEM)
    dma = pltpu.SemaphoreType.DMA
    return pl.pallas_call(
        functools.partial(kernel, nc, nh, modes),
        out_shape=(
            jax.ShapeDtypeStruct((sd, cols), F32),
            jax.ShapeDtypeStruct((sd, nc), F32),
        ),
        in_specs=[vmem] * 5 + [pl.BlockSpec(memory_space=pl.ANY)] * len(consts),
        out_specs=(vmem, vmem),
        scratch_shapes=[pltpu.VMEM(c.shape, c.dtype) for c in consts]
        + [
            pltpu.VMEM((nh, 2, nc, sd), BF16),
            pltpu.VMEM((nh, 2, nc, sd), BF16),
            pltpu.VMEM((nc, rows, sd), BF16),
            pltpu.VMEM((nc, rows, sd), BF16),
            pltpu.VMEM((nc, 1, cb), F32),
            pltpu.VMEM((nc, 1, cb), F32),
            pltpu.VMEM((nc, 1, cb), F32),
            pltpu.VMEM((nc, 1, cb), F32),
            pltpu.VMEM((nc, 1, sd), F32),
            pltpu.VMEM((nc, 1, sd), F32),
            pltpu.VMEM((sd, cols), F32),
            pltpu.VMEM((sd, cols), F32),
            pltpu.VMEM((modes, sd // 8, cb), F32),
            pltpu.VMEM((modes, cols), F32),
            pltpu.VMEM((nc, 1, cb), F32),
            pltpu.VMEM((rows, nc, sd), BF16),
            pltpu.VMEM((4 * nc, 6 * sd), BF16),
            pltpu.VMEM((nc, 2 * sd), F32),
            dma((len(consts),)),
        ]
        + [dma] * 10,
        compiler_params=pltpu.CompilerParams(
            collective_id=0, has_side_effects=True, vmem_limit_bytes=48 * 1024 * 1024
        ),
        name="modal_backward",
    )(inputs, out_grad, decay_rate, residue, skip_gain.reshape(1, cols), *consts)


def solution(mesh):
    placed = (P("ctx", "ch"), P("ctx", "ch"), P(), P(), P("ch"))
    return jax.shard_map(
        functools.partial(body, mesh.shape["ctx"], mesh.shape["ch"]),
        mesh=mesh,
        in_specs=placed,
        out_specs=(P("ctx", "ch"), P("ctx", "ch")),
        check_vma=False,
    )
```

profile of v0, /device:TPU:1, one launch (start us, length us, event | category | flops | bytes accessed | tf_op | source)
XLA Modules:
  0.0 70.0 jit_solution(5820807284418756344)
XLA Ops:
  0.6 0.0 copy-start
  0.6 1.4 %copy-done = bf16[1536,512]{1,0:T(8,128)(2,1)S(1)} copy-done((bf16[1536,512]{1,0:T(8,128)(2,1)S(1)}, bf16[1536,512]{1,0:T(8,128)(2,1)}, u32[]{:S(2)}) %copy-start) | copy-done | bytes 1572888
  2.0 0.0 copy-start.1
  2.0 1.1 %copy-done.1 = bf16[256,1536]{1,0:T(8,128)(2,1)S(1)} copy-done((bf16[256,1536]{1,0:T(8,128)(2,1)S(1)}, bf16[256,1536]{1,0:T(8,128)(2,1)}, u32[]{:S(2)}) %copy-start.1) | copy-done | bytes 786456
  3.2 0.0 copy-start.2
  3.2 1.1 %copy-done.2 = bf16[512,768]{1,0:T(8,128)(2,1)S(1)} copy-done((bf16[512,768]{1,0:T(8,128)(2,1)S(1)}, bf16[512,768]{1,0:T(8,128)(2,1)}, u32[]{:S(2)}) %copy-start.2) | copy-done | bytes 786456
  4.3 0.0 copy-start.3
  4.3 0.9 %copy-done.3 = bf16[256,256]{1,0:T(8,128)(2,1)S(1)} copy-done((bf16[256,256]{1,0:T(8,128)(2,1)S(1)}, bf16[256,256]{1,0:T(8,128)(2,1)}, u32[]{:S(2)}) %copy-start.3) | copy-done | bytes 131096
  5.2 0.0 copy-start.4
  5.2 0.9 %copy-done.4 = bf16[256,512]{1,0:T(8,128)(2,1)S(1)} copy-done((bf16[256,512]{1,0:T(8,128)(2,1)S(1)}, bf16[256,512]{1,0:T(8,128)(2,1)}, u32[]{:S(2)}) %copy-start.4) | copy-done | bytes 262168
  6.2 0.0 copy-start.5
  6.2 0.9 %copy-done.5 = bf16[256,512]{1,0:T(8,128)(2,1)S(1)} copy-done((bf16[256,512]{1,0:T(8,128)(2,1)S(1)}, bf16[256,512]{1,0:T(8,128)(2,1)}, u32[]{:S(2)}) %copy-start.5) | copy-done | bytes 262168
  7.1 0.0 copy-start.6
  7.1 0.9 %copy-done.6 = f32[2,64,256]{2,1,0:T(8,128)S(1)} copy-done((f32[2,64,256]{2,1,0:T(8,128)S(1)}, f32[2,64,256]{2,1,0:T(8,128)}, u32[]{:S(2)}) %copy-start.6) | copy-done | bytes 131096
  8.0 0.0 copy-start.7
  8.0 0.8 %copy-done.7 = bf16[64,384]{1,0:T(8,128)(2,1)S(1)} copy-done((bf16[64,384]{1,0:T(8,128)(2,1)S(1)}, bf16[64,384]{1,0:T(8,128)(2,1)}, u32[]{:S(2)}) %copy-start.7) | copy-done | bytes 49176
  8.8 0.0 copy-start.8
  8.8 0.8 %copy-done.8 = f32[16,512]{1,0:T(8,128)S(1)} copy-done((f32[16,512]{1,0:T(8,128)S(1)}, f32[16,512]{1,0:T(8,128)}, u32[]{:S(2)}) %copy-start.8) | copy-done | bytes 32792
  9.6 0.0 copy-start.9
  9.6 0.8 %copy-done.9 = f32[16,512]{1,0:T(8,128)S(1)} copy-done((f32[16,512]{1,0:T(8,128)S(1)}, f32[16,512]{1,0:T(8,128)}, u32[]{:S(2)}) %copy-start.9) | copy-done | bytes 32792
  10.3 0.0 copy-start.10
  10.3 0.8 %copy-done.10 = bf16[128,128]{1,0:T(8,128)(2,1)S(1)} copy-done((bf16[128,128]{1,0:T(8,128)(2,1)S(1)}, bf16[128,128]{1,0:T(8,128)(2,1)}, u32[]{:S(2)}) %copy-start.10) | copy-done | bytes 32792
  11.1 0.0 copy-start.11
  11.1 0.7 copy-done.11
  11.8 56.7 %modal_backward.1 = (f32[256,512]{1,0:T(8,128)S(1)}, f32[256,64]{1,0:T(8,128)S(1)}) custom-call(bf16[256,512]{1,0:T(8,128)(2,1)S(1)} %copy-done.4, bf16[256,512]{1,0:T(8,128)(2,1)S(1)} %copy-done.5, f32[16,512]{1,0:T(8,128)S(1)} %copy-done.8, f32[16,512]{1,0:T(8,128)S(1)} %copy-done.9, f32[1,512]{1,0:T(1,128)S(1)} %bitcast.1, ...), custom_call_target="tpu_custom_call" | custom-call | tf_op jit(solution)/shard_map/modal_backward/pallas_call | solution.py:325
  68.5 0.7 %copy.15 = f32[256,64]{0,1:T(8,128)} copy(f32[256,64]{1,0:T(8,128)S(1)} %get-tuple-element.3) | data formatting | bytes 131072 | tf_op jit(solution)/shard_map/modal_backward/pallas_call | solution.py:325
  69.2 0.8 %copy.17 = f32[256,512]{1,0:T(8,128)} copy(f32[256,512]{1,0:T(8,128)S(1)} %get-tuple-element.6) | data formatting | bytes 1048576
Async XLA Ops:
  0.6 1.4 %copy-start = (bf16[1536,512]{1,0:T(8,128)(2,1)S(1)}, bf16[1536,512]{1,0:T(8,128)(2,1)}, u32[]{:S(2)}) copy-start(bf16[1536,512]{1,0:T(8,128)(2,1)} %constant.16.clone.refs_8_) | copy-start | bytes 4718596
  2.0 1.1 %copy-start.1 = (bf16[256,1536]{1,0:T(8,128)(2,1)S(1)}, bf16[256,1536]{1,0:T(8,128)(2,1)}, u32[]{:S(2)}) copy-start(bf16[256,1536]{1,0:T(8,128)(2,1)} %constant.20.clone.refs_12_) | copy-start | bytes 2359300
  3.2 1.1 %copy-start.2 = (bf16[512,768]{1,0:T(8,128)(2,1)S(1)}, bf16[512,768]{1,0:T(8,128)(2,1)}, u32[]{:S(2)}) copy-start(bf16[512,768]{1,0:T(8,128)(2,1)} %constant.19.clone.refs_11_) | copy-start | bytes 2359300
  4.3 0.9 %copy-start.3 = (bf16[256,256]{1,0:T(8,128)(2,1)S(1)}, bf16[256,256]{1,0:T(8,128)(2,1)}, u32[]{:S(2)}) copy-start(bf16[256,256]{1,0:T(8,128)(2,1)} %constant.14.clone.refs_5_.refs_6_) | copy-start | bytes 393220
  5.2 0.9 %copy-start.4 = (bf16[256,512]{1,0:T(8,128)(2,1)S(1)}, bf16[256,512]{1,0:T(8,128)(2,1)}, u32[]{:S(2)}) copy-start(bf16[256,512]{1,0:T(8,128)(2,1)} %refs_0_.1) | copy-start | bytes 786436
  6.2 0.9 %copy-start.5 = (bf16[256,512]{1,0:T(8,128)(2,1)S(1)}, bf16[256,512]{1,0:T(8,128)(2,1)}, u32[]{:S(2)}) copy-start(bf16[256,512]{1,0:T(8,128)(2,1)} %refs_1_.1) | copy-start | bytes 786436
  7.1 0.9 %copy-start.6 = (f32[2,64,256]{2,1,0:T(8,128)S(1)}, f32[2,64,256]{2,1,0:T(8,128)}, u32[]{:S(2)}) copy-start(f32[2,64,256]{2,1,0:T(8,128)} %constant.18.clone.refs_10_) | copy-start | bytes 393220
  8.0 0.8 %copy-start.7 = (bf16[64,384]{1,0:T(8,128)(2,1)S(1)}, bf16[64,384]{1,0:T(8,128)(2,1)}, u32[]{:S(2)}) copy-start(bf16[64,384]{1,0:T(8,128)(2,1)} %constant.17.clone.refs_9_) | copy-start | bytes 147460
  8.8 0.8 %copy-start.8 = (f32[16,512]{1,0:T(8,128)S(1)}, f32[16,512]{1,0:T(8,128)}, u32[]{:S(2)}) copy-start(f32[16,512]{1,0:T(8,128)} %refs_2_.1) | copy-start | bytes 98308
  9.6 0.8 %copy-start.9 = (f32[16,512]{1,0:T(8,128)S(1)}, f32[16,512]{1,0:T(8,128)}, u32[]{:S(2)}) copy-start(f32[16,512]{1,0:T(8,128)} %refs_3_.1) | copy-start | bytes 98308
  10.3 0.8 %copy-start.10 = (bf16[128,128]{1,0:T(8,128)(2,1)S(1)}, bf16[128,128]{1,0:T(8,128)(2,1)}, u32[]{:S(2)}) copy-start(bf16[128,128]{1,0:T(8,128)(2,1)} %constant.15.clone.refs_7_) | copy-start | bytes 98308
  11.1 0.7 copy-start.11
where the time goes:
time: 70.6 us; the launch traced here: 70 us
  Pallas kernels  56.7 us (80%)
  local copies, waits for them, and re-layouts  12.6 us (18%)
    pallas_call x1, Pallas kernels, body(): pl.pallas_call(functools.partial(kernel, nc, nh, modes), out_shape=(jax.S...  56.7 us
    unnamed x25, local copies, waits for them, and re-layouts  11.9 us

commit v1 on v0

--- a/solution.py
+++ b/solution.py
@@ -74,13 +74,13 @@
 
 
 def kernel(nc, nh, modes, *refs):
-    (x_ref, g_ref, rate_ref, res_ref, gain_ref), refs = refs[:5], refs[5:]
-    table_in, refs = refs[:8], refs[8:]
+    args_in, refs = refs[:13], refs[13:]
     (y_ref, out_ref), refs = refs[:2], refs[2:]
-    (perm, perm_t, first, second, last, twist, near_in, near_out), refs = refs[:8], refs[8:]
+    args, refs = refs[:13], refs[13:]
+    x_ref, g_ref, rate_ref, res_ref, gain_ref, perm, perm_t, first, second, last, twist, near_in, near_out = args
     (s1, r1, s2, r2, u_own, u_all, st_own, st_all, t_own, t_all), refs = refs[:10], refs[10:]
-    (grad, taps, eb, ww, rate_rows, blocks, left, spec), refs = refs[:8], refs[8:]
-    (table_sem, send1, recv1, send2, recv2, send_u, recv_u, send_s, recv_s, send_t, recv_t) = refs
+    (y, grad, taps, eb, ww, rate_rows, blocks, left, spec), refs = refs[:9], refs[9:]
+    (table_sem, recv1, recv2, y_sem, send1, send2, send_u, recv_u, send_s, recv_s, send_t, recv_t) = refs
 
     sd, cols = x_ref.shape
     rows = 2 * nh
@@ -90,33 +90,52 @@
     me = lax.axis_index("ctx")
     my = lax.axis_index("ch")
 
-    def ctx_peer(k):
-        return lax.rem(me + k, nc)
-
-    def ch_peer(k):
-        return lax.rem(my + k, nh)
+    near = min(nc, 16)
+    spread = nc // near
+    across = min(nh, 4)
+    zs = near // 2
+    far_y = sorted(range(spread), key=lambda d: -min(d, spread - d))
+    far_x = sorted(range(across), key=lambda d: -min(d, across - d))
+    ch_steps = [(d, e) for d in far_x for e in range(nh // across - 1, -1, -1)][:-1]
+    group = me // near
+
+    def group_of(dy):
+        return lax.rem(group + dy, spread)
+
+    def ctx_peer(dy, t):
+        m = t // 2
+        dz = zs // 2 + ((m + 1) // 2) * (2 * (m % 2) - 1) + zs
+        z = lax.rem(lax.rem(me, near) // 2 + dz, zs)
+        core = lax.rem(me + 1 - t % 2, 2)
+        return group_of(dy) * near + z * 2 + core
+
+    def ch_peer(step):
+        dx, dy = step
+        return lax.rem(my // across + dy, nh // across) * across + lax.rem(my + dx, across)
+
+    def each_ctx(dy, act):
+        def body(t, _):
+            act(ctx_peer(dy, t))
+            return 0
+
+        lax.fori_loop(0, near if dy else near - 1, body, 0)
 
     barrier = pltpu.get_barrier_semaphore()
 
-    def greet_ch(k, _):
-        pl.semaphore_signal(barrier, inc=1, device_id={"ch": ch_peer(k)}, device_id_type=MESH)
-        return 0
-
-    def greet_ctx(k, _):
-        pl.semaphore_signal(barrier, inc=1, device_id={"ctx": ctx_peer(k)}, device_id_type=MESH)
-        return 0
-
-    lax.fori_loop(1, nh, greet_ch, 0)
-    lax.fori_loop(1, nc, greet_ctx, 0)
+    def greet(peer):
+        pl.semaphore_signal(barrier, inc=1, device_id={"ctx": peer}, device_id_type=MESH)
 
     loads = [
-        pltpu.make_async_copy(src, dst, table_sem.at[n])
-        for n, (src, dst) in enumerate(
-            zip(table_in, (perm, perm_t, first, second, last, twist, near_in, near_out))
-        )
+        pltpu.make_async_copy(src, dst, table_sem.at[n]) for n, (src, dst) in enumerate(zip(args_in, args))
     ]
     for load in loads:
         load.start()
+
+    for n, dy in enumerate(far_y):
+        each_ctx(dy, greet)
+        if n == 0:
+            for step in ch_steps:
+                pl.semaphore_signal(barrier, inc=1, device_id={"ch": ch_peer(step)}, device_id_type=MESH)
 
     width = min(cols, 256)
     eye = (
@@ -124,27 +143,34 @@
         == lax.broadcasted_iota(jnp.int32, (width, width), 1)
     ).astype(F32).astype(BF16)
     for arr, ref in enumerate((x_ref, g_ref)):
+        loads[arr].wait()
         for c0 in range(0, cols, width):
             turned = lax.dot_general(
                 eye, ref[:, c0 : c0 + width], (((1,), (1,)), ((), ())), preferred_element_type=F32
             ).astype(BF16)
-            turned = turned.reshape(width // nc, nc, sd)
-            for k in range(width // nc):
-                s1[c0 // nc + k, arr] = turned[k]
+            for k in range(width // near):
+                c = c0 + k * near
+                s1[c // nc, c % nc // near, arr] = turned[k * near : (k + 1) * near]
 
     pl.semaphore_wait(barrier, nh - 1 + nc - 1)
 
-    def copy1(k, src, dst):
+    def ch_copy(step, src, dst, n):
         return pltpu.make_async_remote_copy(
-            src_ref=src, dst_ref=dst, send_sem=send1, recv_sem=recv1, device_id={"ch": ch_peer(k)}, device_id_type=MESH
+            src_ref=src,
+            dst_ref=dst,
+            send_sem=send1,
+            recv_sem=recv1.at[n],
+            device_id={"ch": ch_peer(step)},
+            device_id_type=MESH,
         )
 
-    def send_ch(k, _):
-        copy1(k, s1.at[ch_peer(k)], r1.at[my]).start()
-        return 0
-
-    lax.fori_loop(1, nh, send_ch, 0)
+    for n, dy in enumerate(far_y):
+        for step in ch_steps:
+            ch_copy(step, s1.at[ch_peer(step), group_of(dy)], r1.at[my, group_of(dy)], n).start()
     r1[pl.ds(my, 1)] = s1[pl.ds(my, 1)]
+
+    for n in (2, 3, 4):
+        loads[n].wait()
 
     grad[...] = g_ref[...].astype(F32)
     eight = lax.broadcasted_iota(jnp.int32, (8, cb), 0).astype(F32)
@@ -186,32 +212,29 @@
 
     lax.fori_loop(0, nblk, states, 0)
 
-    def ctx_copy(k, src, dst, send, recv):
+    def ctx_copy(peer, src, dst, send, recv):
         return pltpu.make_async_remote_copy(
-            src_ref=src, dst_ref=dst, send_sem=send, recv_sem=recv, device_id={"ctx": ctx_peer(k)}, device_id_type=MESH
+            src_ref=src, dst_ref=dst, send_sem=send, recv_sem=recv, device_id={"ctx": peer}, device_id_type=MESH
         )
 
     def send_to_ctx(own, everyone, send, recv):
-        def body(k, _):
-            ctx_copy(k, own.at[ctx_peer(k)], everyone.at[me], send, recv).start()
-            return 0
-
-        lax.fori_loop(1, nc, body, 0)
+        for dy in far_y:
+            each_ctx(dy, lambda peer: ctx_copy(peer, own.at[peer], everyone.at[me], send, recv).start())
         everyone[pl.ds(me, 1)] = own[pl.ds(me, 1)]
 
-    def wait_ctx(own, everyone, send, recv):
-        return ctx_copy(1, own.at[pl.ds(0, nc - 1)], everyone.at[pl.ds(0, nc - 1)], send, recv)
+    def wait_ctx(own, everyone, send, recv, count=nc - 1):
+        return ctx_copy(ctx_peer(0, 0), own.at[pl.ds(0, count)], everyone.at[pl.ds(0, count)], send, recv)
 
     send_to_ctx(u_own, u_all, send_u, recv_u)
 
-    whole1 = copy1(1, s1.at[pl.ds(0, nh - 1)], r1.at[pl.ds(0, nh - 1)])
-    whole1.wait_recv()
-    loads[0].wait()
-    loads[1].wait()
-    for f0 in range(0, nc, 16):
-        block = r1[:, :, f0 : f0 + 16, :].reshape(rows * 16, sd)
-        s2[f0 : f0 + 16] = dot(perm[...], block).astype(BF16).reshape(16, rows, sd)
-    send_to_ctx(s2, r2, send2, recv2)
+    for n, dy in enumerate(far_y):
+        ch_copy(ch_steps[0], s1.at[pl.ds(0, nh - 1), 0], r1.at[pl.ds(0, nh - 1), 0], n).wait_recv()
+        if n == 0:
+            loads[5].wait()
+        block = r1[:, pl.ds(group_of(dy), 1)].reshape(rows * near, sd)
+        s2[pl.ds(group_of(dy) * near, near)] = dot(perm[...], block).astype(BF16).reshape(near, rows, sd)
+        each_ctx(dy, lambda peer: ctx_copy(peer, s2.at[peer], r2.at[me], send2, recv2.at[group]).start())
+    r2[pl.ds(me, 1)] = s2[pl.ds(me, 1)]
 
     wait_ctx(u_own, u_all, send_u, recv_u).wait_recv()
     decay = jnp.exp(-rate_rows[me] * float(sd))
@@ -221,8 +244,8 @@
         state = u_all[p] + decay * state
     send_to_ctx(st_own, st_all, send_s, recv_s)
 
-    loads[6].wait()
-    loads[7].wait()
+    loads[11].wait()
+    loads[12].wait()
     wide = min(cols, 256)
 
     def inside(blk, _):
@@ -235,45 +258,25 @@
         h_re, h_im = h_spec[:sd], h_spec[sd:]
         term = jnp.concatenate([h_re * g_re + h_im * g_im, h_re * g_im - h_im * g_re], axis=0)
         high, low = split(term)
-        near = dot(near_out[...], jnp.concatenate([high, low, high], axis=0)) * (1.0 / sd)
-        y_ref[:, at] = near + gain_ref[:, at] * grad[:, at]
+        part = dot(near_out[...], jnp.concatenate([high, low, high], axis=0)) * (1.0 / sd)
+        y[:, at] = part + gain_ref[:, at] * grad[:, at]
         return 0
 
     lax.fori_loop(0, cols // wide, inside, 0)
 
-    wait_ctx(st_own, st_all, send_s, recv_s).wait_recv()
-
-    def outside(blk, _):
-        at = columns(blk)
-        rate = rate_ref[:, at]
-        weight = ww[:, at]
-        fine = []
-        for n in range(modes):
-            carried = weight[n : n + 1] * st_all[n * nblk + blk]
-            eb[n] = carried * jnp.exp(-rate[n : n + 1] * (float(sd - 8) - octs))
-            fine.append(jnp.exp(-rate[n : n + 1] * (8.0 - eight)))
-        for t in range(tiles):
-            total = y_ref[8 * t : 8 * t + 8, at]
-            for n in range(modes):
-                total = total + jnp.broadcast_to(eb[n, t : t + 1], (8, cb)) * fine[n]
-            y_ref[8 * t : 8 * t + 8, at] = total
-        return 0
-
-    lax.fori_loop(0, nblk, outside, 0)
-
-    for n in (2, 3, 4, 5):
+    for n in (6, 7, 8, 9, 10):
         loads[n].wait()
-    wait_ctx(s2, r2, send2, recv2).wait_recv()
-    for a0 in range(0, nc, 16):
-        block = r2[a0 : a0 + 16].reshape(16 * rows, sd)
-        blocks[:, a0 : a0 + 16, :] = dot(perm_t[...], block).astype(BF16).reshape(rows, 16, sd)
+    for dy in reversed(far_y):
+        wait_ctx(s2, r2, send2, recv2.at[group_of(dy)], near if dy else near - 1).wait_recv()
+        block = r2[pl.ds(group_of(dy) * near, near)].reshape(near * rows, sd)
+        blocks[pl.ds(group_of(dy), 1)] = dot(perm_t[...], block).astype(BF16).reshape(1, rows, near, sd)
     turn_c, turn_s = twist[0], twist[1]
     spec[...] = jnp.zeros_like(spec)
 
     def pair(q, _):
         for k in range(4):
-            part = blocks[4 * q + k]
-            freq = dot(first[...], jnp.concatenate([part, part], axis=0))
+            part = [blocks[a, 4 * q + k] for a in range(spread)]
+            freq = dot(first[...], jnp.concatenate(part + part, axis=0))
             re, im = freq[:nc], freq[nc:]
             high_re, low_re = split(re * turn_c + im * turn_s)
             high_im, low_im = split(im * turn_c - re * turn_s)
@@ -303,12 +306,37 @@
     for d in range(nc):
         t_own[d] = result[d : d + 1]
     send_to_ctx(t_own, t_all, send_t, recv_t)
+
+    wait_ctx(st_own, st_all, send_s, recv_s).wait_recv()
+
+    def outside(blk, _):
+        at = columns(blk)
+        rate = rate_ref[:, at]
+        weight = ww[:, at]
+        fine = []
+        for n in range(modes):
+            carried = weight[n : n + 1] * st_all[n * nblk + blk]
+            eb[n] = carried * jnp.exp(-rate[n : n + 1] * (float(sd - 8) - octs))
+            fine.append(jnp.exp(-rate[n : n + 1] * (8.0 - eight)))
+        for t in range(tiles):
+            total = y[8 * t : 8 * t + 8, at]
+            for n in range(modes):
+                total = total + jnp.broadcast_to(eb[n, t : t + 1], (8, cb)) * fine[n]
+            y[8 * t : 8 * t + 8, at] = total
+        return 0
+
+    lax.fori_loop(0, nblk, outside, 0)
+
+    leave = pltpu.make_async_copy(y, y_ref, y_sem)
+    leave.start()
+
     wait_ctx(t_own, t_all, send_t, recv_t).wait_recv()
     gathered = jnp.concatenate([t_all[d] for d in range(nc)], axis=0)
-    out_ref[...] = gathered.T
-
-    whole1.wait_send()
-    wait_ctx(s2, r2, send2, recv2).wait_send()
+    out_ref[...] = gathered
+
+    leave.wait()
+    ch_copy(ch_steps[0], s1.at[pl.ds(0, nh - 1)], r1.at[pl.ds(0, nh - 1)], 0).wait_send()
+    wait_ctx(s2, r2, send2, recv2.at[0]).wait_send()
     wait_ctx(u_own, u_all, send_u, recv_u).wait_send()
     wait_ctx(st_own, st_all, send_s, recv_s).wait_send()
     wait_ctx(t_own, t_all, send_t, recv_t).wait_send()
@@ -319,21 +347,24 @@
     modes = decay_rate.shape[0]
     rows = 2 * nh
     cb = modes * cols // nc
-    consts = [jnp.asarray(t) for t in tables(nc, nh, sd)]
+    args = (inputs, out_grad, decay_rate, residue, skip_gain.reshape(1, cols))
+    args += tuple(jnp.asarray(t) for t in tables(nc, nh, sd))
+    near = min(nc, 16)
+    spread = nc // near
     vmem = pl.BlockSpec(memory_space=pltpu.VMEM)
     dma = pltpu.SemaphoreType.DMA
-    return pl.pallas_call(
+    input_grad, filter_grad = pl.pallas_call(
         functools.partial(kernel, nc, nh, modes),
         out_shape=(
             jax.ShapeDtypeStruct((sd, cols), F32),
-            jax.ShapeDtypeStruct((sd, nc), F32),
+            jax.ShapeDtypeStruct((nc, sd), F32),
         ),
-        in_specs=[vmem] * 5 + [pl.BlockSpec(memory_space=pl.ANY)] * len(consts),
-        out_specs=(vmem, vmem),
-        scratch_shapes=[pltpu.VMEM(c.shape, c.dtype) for c in consts]
+        in_specs=[pl.BlockSpec(memory_space=pltpu.HBM)] * len(args),
+        out_specs=(pl.BlockSpec(memory_space=pltpu.HBM), vmem),
+        scratch_shapes=[pltpu.VMEM(arg.shape, arg.dtype) for arg in args]
         + [
-            pltpu.VMEM((nh, 2, nc, sd), BF16),
-            pltpu.VMEM((nh, 2, nc, sd), BF16),
+            pltpu.VMEM((nh, spread, 2, near, sd), BF16),
+            pltpu.VMEM((nh, spread, 2, near, sd), BF16),
             pltpu.VMEM((nc, rows, sd), BF16),
             pltpu.VMEM((nc, rows, sd), BF16),
             pltpu.VMEM((nc, 1, cb), F32),
@@ -344,20 +375,24 @@
             pltpu.VMEM((nc, 1, sd), F32),
             pltpu.VMEM((sd, cols), F32),
             pltpu.VMEM((sd, cols), F32),
+            pltpu.VMEM((sd, cols), F32),
             pltpu.VMEM((modes, sd // 8, cb), F32),
             pltpu.VMEM((modes, cols), F32),
             pltpu.VMEM((nc, 1, cb), F32),
-            pltpu.VMEM((rows, nc, sd), BF16),
+            pltpu.VMEM((spread, rows, near, sd), BF16),
             pltpu.VMEM((4 * nc, 6 * sd), BF16),
             pltpu.VMEM((nc, 2 * sd), F32),
-            dma((len(consts),)),
+            dma((len(args),)),
+            dma((spread,)),
+            dma((spread,)),
         ]
-        + [dma] * 10,
+        + [dma] * 9,
         compiler_params=pltpu.CompilerParams(
-            collective_id=0, has_side_effects=True, vmem_limit_bytes=48 * 1024 * 1024
+            collective_id=0, has_side_effects=True, vmem_limit_bytes=64 * 1024 * 1024
         ),
         name="modal_backward",
-    )(inputs, out_grad, decay_rate, residue, skip_gain.reshape(1, cols), *consts)
+    )(*args)
+    return input_grad, filter_grad.T
 
 
 def solution(mesh):

time: 70.6 us -> 56.4 us (0.80)
  local copies, waits for them, and re-layouts: 12.6 us -> 3.34 us
  Pallas kernels: 56.7 us -> 52.2 us
    unnamed x25 -> x2, local copies, waits for them, and re-layouts: 11.9 us -> 3.34 us
    pallas_call x1, Pallas kernels: 56.7 us -> 52.2 us  [body(): pl.pallas_call(functools.partial(kernel, nc, nh, modes), out_shape=(jax.S...]
    pallas_call x1 -> x0, local copies, waits for them, and re-layouts: 0.71 us -> none  [body(): pl.pallas_call(functools.partial(kernel, nc, nh, modes), out_shape=(jax.S...]
where the time goes in v1:
time: 56.4 us; the launch traced here: 56.1 us
  Pallas kernels  52.2 us (93%)
  local copies, waits for them, and re-layouts  3.34 us (6%)
  between operations  0.64 us (1%)
    pallas_call x1, Pallas kernels, body(): pl.pallas_call(functools.partial(kernel, nc, nh, modes), out_shape=(jax.S...  52.2 us
    unnamed x2, local copies, waits for them, and re-layouts  3.34 us

profile of v1, /device:TPU:1, one launch (start us, length us, event | category | flops | bytes accessed | tf_op | source)
XLA Modules:
  0.0 56.1 jit_solution(14216932938615739827)
XLA Ops:
  0.6 52.2 %modal_backward.1 = (f32[256,512]{1,0:T(8,128)}, f32[64,256]{1,0:T(8,128)}) custom-call(bf16[256,512]{1,0:T(8,128)(2,1)} %refs_0_.1, bf16[256,512]{1,0:T(8,128)(2,1)} %refs_1_.1, f32[16,512]{1,0:T(8,128)} %refs_2_.1, f32[16,512]{1,0:T(8,128)} %refs_3_.1, f32[1,512]{1,0:T(1,128)} %bitcast.3, bf16[256,256]{1,0:T(8,128)(2,1)} %constant.14.clone.refs_5_.refs_6_, ...), custom_call_target="tpu_custom_call" | custom-call | tf_op jit(solution)/shard_map/modal_backward/pallas_call | solution.py:356
  52.8 1.9 %copy.17 = f32[256,512]{1,0:T(8,128)} copy(f32[256,512]{1,0:T(8,128)} %get-tuple-element.8) | data formatting | bytes 1048576
  54.7 1.5 %copy.18 = f32[256,64]{0,1:T(8,128)} copy(f32[256,64]{0,1:T(8,128)} %bitcast.2) | data formatting | bytes 131072

commit v2 on v1

--- a/solution.py
+++ b/solution.py
@@ -15,6 +15,12 @@
 BF16 = jnp.bfloat16
 
 
+def shape_of(nc, nh):
+    z = nc // 8 if nc >= 32 else nc // 4
+    x = nh // 2
+    return nc // (2 * z), z, 2, nh // x, x
+
+
 def halves(table):
     high = table.astype(np.float32).astype(ml_dtypes.bfloat16)
     low = (table - high.astype(np.float64)).astype(np.float32).astype(ml_dtypes.bfloat16)
@@ -23,7 +29,7 @@
 
 @functools.lru_cache(maxsize=None)
 def tables(nc, nh, sd):
-    rows = 2 * nh
+    _, zs, cores, _, xs = shape_of(nc, nh)
     j = np.arange(nc) + 0.5
     a = np.arange(nc)
     s = np.arange(sd)
@@ -46,15 +52,19 @@
     high, low = halves(near)
     near_in = np.concatenate([high, low, high], axis=1)
     near_out = np.concatenate([high.T, high.T, low.T], axis=1)
-    size = 16 * rows
-    perm = np.zeros((size, size), np.float32)
-    for f in range(16):
-        for r in range(rows):
-            perm[f * rows + r, r * 16 + f] = 1.0
+    rows = cores * xs * 2
+    gather = np.zeros((zs * rows, zs * rows), np.float32)
+    spread = np.zeros((zs * rows, zs * rows), np.float32)
+    for z in range(zs):
+        for q in range(cores * xs):
+            for arr in range(2):
+                gather[(z * cores * xs + q) * 2 + arr, (q * 2 + arr) * zs + z] = 1.0
+                core, x = q // xs, q % xs
+                spread[((x * 2 + arr) * zs + z) * cores + core, (z * cores * xs + q) * 2 + arr] = 1.0
     bf = ml_dtypes.bfloat16
     return (
-        perm.astype(bf),
-        perm.T.copy().astype(bf),
+        gather.astype(bf),
+        spread.astype(bf),
         first,
         np.ascontiguousarray(second),
         last,
@@ -77,53 +87,67 @@
     args_in, refs = refs[:13], refs[13:]
     (y_ref, out_ref), refs = refs[:2], refs[2:]
     args, refs = refs[:13], refs[13:]
-    x_ref, g_ref, rate_ref, res_ref, gain_ref, perm, perm_t, first, second, last, twist, near_in, near_out = args
+    x_ref, g_ref, rate_ref, res_ref, gain_ref, gather, spread, first, second, last, twist, near_in, near_out = args
     (s1, r1, s2, r2, u_own, u_all, st_own, st_all, t_own, t_all), refs = refs[:10], refs[10:]
     (y, grad, taps, eb, ww, rate_rows, blocks, left, spec), refs = refs[:9], refs[9:]
     (table_sem, recv1, recv2, y_sem, send1, send2, send_u, recv_u, send_s, recv_s, send_t, recv_t) = refs
 
     sd, cols = x_ref.shape
-    rows = 2 * nh
     cb = modes * cols // nc
     nblk = cols // cb
     tiles = sd // 8
+    yhs, zs, cores, yls, xs = shape_of(nc, nh)
+    ys, qs, run = yhs * yls, cores * xs, zs * cores
     me = lax.axis_index("ctx")
     my = lax.axis_index("ch")
-
-    near = min(nc, 16)
-    spread = nc // near
-    across = min(nh, 4)
-    zs = near // 2
-    far_y = sorted(range(spread), key=lambda d: -min(d, spread - d))
-    far_x = sorted(range(across), key=lambda d: -min(d, across - d))
-    ch_steps = [(d, e) for d in far_x for e in range(nh // across - 1, -1, -1)][:-1]
-    group = me // near
-
-    def group_of(dy):
-        return lax.rem(group + dy, spread)
-
-    def ctx_peer(dy, t):
-        m = t // 2
-        dz = zs // 2 + ((m + 1) // 2) * (2 * (m % 2) - 1) + zs
-        z = lax.rem(lax.rem(me, near) // 2 + dz, zs)
-        core = lax.rem(me + 1 - t % 2, 2)
-        return group_of(dy) * near + z * 2 + core
-
-    def ch_peer(step):
-        dx, dy = step
-        return lax.rem(my // across + dy, nh // across) * across + lax.rem(my + dx, across)
-
-    def each_ctx(dy, act):
+    yh, z, core = me // run, lax.rem(me, run) // cores, lax.rem(me, cores)
+    yl, x = my // xs, lax.rem(my, xs)
+    y_me = yh * yls + yl
+    q_me = core * xs + x
+
+    def farthest(count):
+        return sorted(range(count), key=lambda d: -min(d, count - d))
+
+    far_y = farthest(ys)
+    q_steps = [(dc, dx) for dx in farthest(xs) for dc in (1, 0)][:-1]
+
+    def z_at(m):
+        return lax.rem(z + zs // 2 + ((m + 1) // 2) * (2 * lax.rem(m, 2) - 1) + zs, zs)
+
+    def y_at(dy):
+        return lax.rem(y_me + dy, ys)
+
+    def plane_peer(dy, m):
+        there = y_at(dy)
+        device = {"ctx": (there // yls * zs + z_at(m)) * cores + core, "ch": lax.rem(there, yls) * xs + x}
+        return device, there * zs + z_at(m)
+
+    def chip_peer(step):
+        dc, dx = step
+        core_at, x_at = lax.rem(core + dc, cores), lax.rem(x + dx, xs)
+        return {"ctx": me - core + core_at, "ch": yl * xs + x_at}, core_at * xs + x_at
+
+    def ctx_peer(dyh, t):
+        return (lax.rem(yh + dyh, yhs) * zs + z_at(t // cores)) * cores + lax.rem(core + 1 - lax.rem(t, cores), cores)
+
+    def each_plane(dy, act):
+        def body(m, _):
+            act(*plane_peer(dy, m))
+            return 0
+
+        lax.fori_loop(0, zs if dy else zs - 1, body, 0)
+
+    def each_ctx(dyh, act):
         def body(t, _):
-            act(ctx_peer(dy, t))
+            act(ctx_peer(dyh, t))
             return 0
 
-        lax.fori_loop(0, near if dy else near - 1, body, 0)
+        lax.fori_loop(0, run if dyh else run - 1, body, 0)
 
     barrier = pltpu.get_barrier_semaphore()
 
-    def greet(peer):
-        pl.semaphore_signal(barrier, inc=1, device_id={"ctx": peer}, device_id_type=MESH)
+    def greet(device, _):
+        pl.semaphore_signal(barrier, inc=1, device_id=device, device_id_type=MESH)
 
     loads = [
         pltpu.make_async_copy(src, dst, table_sem.at[n]) for n, (src, dst) in enumerate(zip(args_in, args))
@@ -132,42 +156,53 @@
         load.start()
 
     for n, dy in enumerate(far_y):
-        each_ctx(dy, greet)
-        if n == 0:
-            for step in ch_steps:
-                pl.semaphore_signal(barrier, inc=1, device_id={"ch": ch_peer(step)}, device_id_type=MESH)
+        each_plane(dy, greet)
+        if n == 2:
+            for step in q_steps:
+                greet(*chip_peer(step))
+
+    for dyh in farthest(yhs):
+        def other(m, _):
+            device = (lax.rem(yh + dyh, yhs) * zs + z_at(m)) * cores + lax.rem(core + 1, cores)
+            greet({"ctx": device}, 0)
+            return 0
+
+        lax.fori_loop(0, zs if dyh else zs - 1, other, 0)
 
     width = min(cols, 256)
-    eye = (
-        lax.broadcasted_iota(jnp.int32, (width, width), 0)
+    row = lax.broadcasted_iota(jnp.int32, (width, width), 0)
+    turn = (
+        (row & -run) + (row & (zs - 1)) * cores + ((row & (run - 1)) // zs)
         == lax.broadcasted_iota(jnp.int32, (width, width), 1)
     ).astype(F32).astype(BF16)
-    for arr, ref in enumerate((x_ref, g_ref)):
-        loads[arr].wait()
-        for c0 in range(0, cols, width):
-            turned = lax.dot_general(
-                eye, ref[:, c0 : c0 + width], (((1,), (1,)), ((), ())), preferred_element_type=F32
-            ).astype(BF16)
-            for k in range(width // near):
-                c = c0 + k * near
-                s1[c // nc, c % nc // near, arr] = turned[k * near : (k + 1) * near]
-
-    pl.semaphore_wait(barrier, nh - 1 + nc - 1)
-
-    def ch_copy(step, src, dst, n):
+    loads[0].wait()
+    loads[1].wait()
+    for c0 in range(0, cols, width):
+        pair_of = [
+            lax.dot_general(turn, ref[:, c0 : c0 + width], (((1,), (1,)), ((), ())), preferred_element_type=F32)
+            for ref in (x_ref, g_ref)
+        ]
+        for r0 in range(0, width, zs):
+            c = c0 + r0
+            to_core = c % run // zs
+            to_yh = c // run % yhs
+            to_yl, to_x = c // nc // xs, c // nc % xs
+            both = jnp.concatenate([part[r0 : r0 + zs] for part in pair_of], axis=0)
+            s1[to_core * xs + to_x, to_yh * yls + to_yl] = both.astype(BF16)
+
+    pl.semaphore_wait(barrier, (ys * zs - 1) + (qs - 1) + (yhs * zs - 1))
+
+    def copy(device, src, dst, send, recv):
         return pltpu.make_async_remote_copy(
-            src_ref=src,
-            dst_ref=dst,
-            send_sem=send1,
-            recv_sem=recv1.at[n],
-            device_id={"ch": ch_peer(step)},
-            device_id_type=MESH,
+            src_ref=src, dst_ref=dst, send_sem=send, recv_sem=recv, device_id=device, device_id_type=MESH
         )
 
+    some_chip, _ = chip_peer(q_steps[0])
     for n, dy in enumerate(far_y):
-        for step in ch_steps:
-            ch_copy(step, s1.at[ch_peer(step), group_of(dy)], r1.at[my, group_of(dy)], n).start()
-    r1[pl.ds(my, 1)] = s1[pl.ds(my, 1)]
+        for step in q_steps:
+            device, q_at = chip_peer(step)
+            copy(device, s1.at[q_at, y_at(dy)], r1.at[q_me, y_at(dy)], send1, recv1.at[n]).start()
+    r1[pl.ds(q_me, 1)] = s1[pl.ds(q_me, 1)]
 
     for n in (2, 3, 4):
         loads[n].wait()
@@ -213,13 +248,11 @@
     lax.fori_loop(0, nblk, states, 0)
 
     def ctx_copy(peer, src, dst, send, recv):
-        return pltpu.make_async_remote_copy(
-            src_ref=src, dst_ref=dst, send_sem=send, recv_sem=recv, device_id={"ctx": peer}, device_id_type=MESH
-        )
+        return copy({"ctx": peer}, src, dst, send, recv)
 
     def send_to_ctx(own, everyone, send, recv):
-        for dy in far_y:
-            each_ctx(dy, lambda peer: ctx_copy(peer, own.at[peer], everyone.at[me], send, recv).start())
+        for dyh in farthest(yhs):
+            each_ctx(dyh, lambda peer: ctx_copy(peer, own.at[peer], everyone.at[me], send, recv).start())
         everyone[pl.ds(me, 1)] = own[pl.ds(me, 1)]
 
     def wait_ctx(own, everyone, send, recv, count=nc - 1):
@@ -228,13 +261,18 @@
     send_to_ctx(u_own, u_all, send_u, recv_u)
 
     for n, dy in enumerate(far_y):
-        ch_copy(ch_steps[0], s1.at[pl.ds(0, nh - 1), 0], r1.at[pl.ds(0, nh - 1), 0], n).wait_recv()
+        copy(some_chip, s1.at[pl.ds(0, qs - 1), 0], r1.at[pl.ds(0, qs - 1), 0], send1, recv1.at[n]).wait_recv()
         if n == 0:
             loads[5].wait()
-        block = r1[:, pl.ds(group_of(dy), 1)].reshape(rows * near, sd)
-        s2[pl.ds(group_of(dy) * near, near)] = dot(perm[...], block).astype(BF16).reshape(near, rows, sd)
-        each_ctx(dy, lambda peer: ctx_copy(peer, s2.at[peer], r2.at[me], send2, recv2.at[group]).start())
-    r2[pl.ds(me, 1)] = s2[pl.ds(me, 1)]
+        block = r1[:, pl.ds(y_at(dy), 1)].reshape(qs * 2 * zs, sd)
+        s2[pl.ds(y_at(dy) * zs, zs)] = dot(gather[...], block).astype(BF16).reshape(zs, qs * 2, sd)
+
+        def onward(device, at):
+            copy(device, s2.at[at], r2.at[y_me * zs + z], send2, recv2.at[y_me]).start()
+
+        each_plane(dy, onward)
+    own = pl.ds(y_me * zs + z, 1)
+    r2[own] = s2[own]
 
     wait_ctx(u_own, u_all, send_u, recv_u).wait_recv()
     decay = jnp.exp(-rate_rows[me] * float(sd))
@@ -266,16 +304,22 @@
 
     for n in (6, 7, 8, 9, 10):
         loads[n].wait()
+    some_plane, _ = plane_peer(far_y[0], 0)
     for dy in reversed(far_y):
-        wait_ctx(s2, r2, send2, recv2.at[group_of(dy)], near if dy else near - 1).wait_recv()
-        block = r2[pl.ds(group_of(dy) * near, near)].reshape(near * rows, sd)
-        blocks[pl.ds(group_of(dy), 1)] = dot(perm_t[...], block).astype(BF16).reshape(1, rows, near, sd)
+        count = zs if dy else zs - 1
+        copy(
+            some_plane, s2.at[pl.ds(0, count)], r2.at[pl.ds(0, count)], send2, recv2.at[y_at(dy)]
+        ).wait_recv()
+        block = r2[pl.ds(y_at(dy) * zs, zs)].reshape(zs * qs * 2, sd)
+        blocks[pl.ds(y_at(dy), 1)] = dot(spread[...], block).astype(BF16).reshape(1, xs * 2, run, sd)
     turn_c, turn_s = twist[0], twist[1]
     spec[...] = jnp.zeros_like(spec)
 
     def pair(q, _):
         for k in range(4):
-            part = [blocks[a, 4 * q + k] for a in range(spread)]
+            share = 2 * q + k // 2
+            at = lax.rem(share, xs) * 2 + k % 2
+            part = [blocks[a * yls + share // xs, at] for a in range(yhs)]
             freq = dot(first[...], jnp.concatenate(part + part, axis=0))
             re, im = freq[:nc], freq[nc:]
             high_re, low_re = split(re * turn_c + im * turn_s)
@@ -335,22 +379,27 @@
     out_ref[...] = gathered
 
     leave.wait()
-    ch_copy(ch_steps[0], s1.at[pl.ds(0, nh - 1)], r1.at[pl.ds(0, nh - 1)], 0).wait_send()
-    wait_ctx(s2, r2, send2, recv2.at[0]).wait_send()
+    copy(some_chip, s1.at[pl.ds(0, qs - 1)], r1.at[pl.ds(0, qs - 1)], send1, recv1.at[0]).wait_send()
+    rest = pl.ds(0, ys * zs - 1)
+    copy(some_plane, s2.at[rest], r2.at[rest], send2, recv2.at[0]).wait_send()
     wait_ctx(u_own, u_all, send_u, recv_u).wait_send()
     wait_ctx(st_own, st_all, send_s, recv_s).wait_send()
     wait_ctx(t_own, t_all, send_t, recv_t).wait_send()
 
 
+def finish(input_in, filter_in, input_out, filter_out):
+    input_out[...] = input_in[...]
+    filter_out[...] = filter_in[...]
+
+
 def body(nc, nh, inputs, out_grad, decay_rate, residue, skip_gain):
     sd, cols = inputs.shape
     modes = decay_rate.shape[0]
-    rows = 2 * nh
     cb = modes * cols // nc
     args = (inputs, out_grad, decay_rate, residue, skip_gain.reshape(1, cols))
     args += tuple(jnp.asarray(t) for t in tables(nc, nh, sd))
-    near = min(nc, 16)
-    spread = nc // near
+    yhs, zs, cores, yls, xs = shape_of(nc, nh)
+    ys, qs = yhs * yls, cores * xs
     vmem = pl.BlockSpec(memory_space=pltpu.VMEM)
     dma = pltpu.SemaphoreType.DMA
     input_grad, filter_grad = pl.pallas_call(
@@ -363,10 +412,10 @@
         out_specs=(pl.BlockSpec(memory_space=pltpu.HBM), vmem),
         scratch_shapes=[pltpu.VMEM(arg.shape, arg.dtype) for arg in args]
         + [
-            pltpu.VMEM((nh, spread, 2, near, sd), BF16),
-            pltpu.VMEM((nh, spread, 2, near, sd), BF16),
-            pltpu.VMEM((nc, rows, sd), BF16),
-            pltpu.VMEM((nc, rows, sd), BF16),
+            pltpu.VMEM((qs, ys, 2 * zs, sd), BF16),
+            pltpu.VMEM((qs, ys, 2 * zs, sd), BF16),
+            pltpu.VMEM((ys * zs, qs * 2, sd), BF16),
+            pltpu.VMEM((ys * zs, qs * 2, sd), BF16),
             pltpu.VMEM((nc, 1, cb), F32),
             pltpu.VMEM((nc, 1, cb), F32),
             pltpu.VMEM((nc, 1, cb), F32),
@@ -379,12 +428,12 @@
             pltpu.VMEM((modes, sd // 8, cb), F32),
             pltpu.VMEM((modes, cols), F32),
             pltpu.VMEM((nc, 1, cb), F32),
-            pltpu.VMEM((spread, rows, near, sd), BF16),
+            pltpu.VMEM((ys, xs * 2, zs * cores, sd), BF16),
             pltpu.VMEM((4 * nc, 6 * sd), BF16),
             pltpu.VMEM((nc, 2 * sd), F32),
             dma((len(args),)),
-            dma((spread,)),
-            dma((spread,)),
+            dma((ys,)),
+            dma((ys,)),
         ]
         + [dma] * 9,
         compiler_params=pltpu.CompilerParams(
@@ -392,6 +441,14 @@
         ),
         name="modal_backward",
     )(*args)
+    input_grad, filter_grad = pl.pallas_call(
+        finish,
+        out_shape=(jax.ShapeDtypeStruct((sd, cols), F32), jax.ShapeDtypeStruct((nc, sd), F32)),
+        in_specs=[vmem, vmem],
+        out_specs=(vmem, vmem),
+        compiler_params=pltpu.CompilerParams(vmem_limit_bytes=64 * 1024 * 1024),
+        name="finish",
+    )(input_grad, filter_grad)
     return input_grad, filter_grad.T
 
 

time: 56.4 us -> 55.7 us (0.988)
  local copies, waits for them, and re-layouts: 3.34 us -> 0 us
  Pallas kernels: 52.2 us -> 54.9 us
    unnamed x2 -> x0, local copies, waits for them, and re-layouts: 3.34 us -> none
    pallas_call x0 -> x1, Pallas kernels: none -> 1.88 us  [body(): pl.pallas_call(finish, out_shape=(jax.ShapeDtypeStruct((sd, cols), F32),...]
    pallas_call x1, Pallas kernels: 52.2 us -> 53.1 us  [body(): pl.pallas_call(functools.partial(kernel, nc, nh, modes), out_shape=(jax.S...]
where the time goes in v2:
time: 55.7 us; the launch traced here: 55.6 us
  Pallas kernels  54.9 us (99%)
  between operations  0.64 us (1%)
    pallas_call x1, Pallas kernels, body(): pl.pallas_call(functools.partial(kernel, nc, nh, modes), out_shape=(jax.S...  53.1 us
    pallas_call x1, Pallas kernels, body(): pl.pallas_call(finish, out_shape=(jax.ShapeDtypeStruct((sd, cols), F32),...  1.88 us

profile of v2, /device:TPU:1, one launch (start us, length us, event | category | flops | bytes accessed | tf_op | source)
XLA Modules:
  0.0 55.6 jit_solution(6939267535165989298)
XLA Ops:
  0.6 53.1 %modal_backward.1 = (f32[256,512]{1,0:T(8,128)}, f32[64,256]{1,0:T(8,128)}) custom-call(bf16[256,512]{1,0:T(8,128)(2,1)} %refs_0_.1, bf16[256,512]{1,0:T(8,128)(2,1)} %refs_1_.1, f32[16,512]{1,0:T(8,128)} %refs_2_.1, f32[16,512]{1,0:T(8,128)} %refs_3_.1, f32[1,512]{1,0:T(1,128)} %bitcast.2, bf16[128,128]{1,0:T(8,128)(2,1)} %constant.14.clone.refs_5_.refs_6_, ...), custom_call_target="tpu_custom_call" | custom-call | tf_op jit(solution)/shard_map/modal_backward/pallas_call | solution.py:405
  53.7 1.9 %finish.1 = (f32[256,512]{1,0:T(8,128)}, f32[64,256]{1,0:T(8,128)}) custom-call(f32[256,512]{1,0:T(8,128)} %get-tuple-element.6.input_in, f32[64,256]{1,0:T(8,128)} %get-tuple-element.7.filter_in), custom_call_target="tpu_custom_call" | custom-call | tf_op jit(solution)/shard_map/finish/pallas_call | solution.py:444

commit v3 on v2

--- a/solution.py
+++ b/solution.py
@@ -25,6 +25,12 @@
     high = table.astype(np.float32).astype(ml_dtypes.bfloat16)
     low = (table - high.astype(np.float64)).astype(np.float32).astype(ml_dtypes.bfloat16)
     return high, low
+
+
+def reorder(sizes, old, new):
+    count = np.arange(math.prod(sizes[axis] for axis in old)).reshape([sizes[axis] for axis in old])
+    moved = count.transpose([old.index(axis) for axis in new]).reshape(-1)
+    return np.eye(moved.size, dtype=np.float32)[moved]
 
 
 @functools.lru_cache(maxsize=None)
@@ -52,19 +58,17 @@
     high, low = halves(near)
     near_in = np.concatenate([high, low, high], axis=1)
     near_out = np.concatenate([high.T, high.T, low.T], axis=1)
-    rows = cores * xs * 2
-    gather = np.zeros((zs * rows, zs * rows), np.float32)
-    spread = np.zeros((zs * rows, zs * rows), np.float32)
-    for z in range(zs):
-        for q in range(cores * xs):
-            for arr in range(2):
-                gather[(z * cores * xs + q) * 2 + arr, (q * 2 + arr) * zs + z] = 1.0
-                core, x = q // xs, q % xs
-                spread[((x * 2 + arr) * zs + z) * cores + core, (z * cores * xs + q) * 2 + arr] = 1.0
+    qx = {"q": cores * xs, "core": cores, "x": xs, "arr": 2, "z": zs}
+    moves = [
+        reorder(qx, ("core", "x", "arr", "z"), ("z", "core", "x", "arr")),
+        reorder(qx, ("z", "core", "x", "arr"), ("x", "arr", "z", "core")),
+        reorder(qx, ("arr", "x", "core", "z"), ("z", "arr", "core", "x")),
+        reorder(qx, ("z", "arr", "core", "x"), ("core", "x", "arr", "z")),
+        reorder(qx, ("core", "x", "arr", "z"), ("x", "arr", "z", "core")),
+    ]
     bf = ml_dtypes.bfloat16
     return (
-        gather.astype(bf),
-        spread.astype(bf),
+        np.stack(moves).astype(bf),
         first,
         np.ascontiguousarray(second),
         last,
@@ -84,13 +88,14 @@
 
 
 def kernel(nc, nh, modes, *refs):
-    args_in, refs = refs[:13], refs[13:]
+    args_in, refs = refs[:12], refs[12:]
     (y_ref, out_ref), refs = refs[:2], refs[2:]
-    args, refs = refs[:13], refs[13:]
-    x_ref, g_ref, rate_ref, res_ref, gain_ref, gather, spread, first, second, last, twist, near_in, near_out = args
-    (s1, r1, s2, r2, u_own, u_all, st_own, st_all, t_own, t_all), refs = refs[:10], refs[10:]
+    args, refs = refs[:12], refs[12:]
+    x_ref, g_ref, rate_ref, res_ref, gain_ref, moves, first, second, last, twist, near_in, near_out = args
+    (runs, s1, r1, s2, r2, s3, r3, s4, r4), refs = refs[:9], refs[9:]
+    (u_own, u_all, st_own, st_all, t_own, t_all), refs = refs[:6], refs[6:]
     (y, grad, taps, eb, ww, rate_rows, blocks, left, spec), refs = refs[:9], refs[9:]
-    (table_sem, recv1, recv2, y_sem, send1, send2, send_u, recv_u, send_s, recv_s, send_t, recv_t) = refs
+    (table_sem, recv1, recv2, recv3, recv4, y_sem, send1, send2, send3, send4, send_u, recv_u, send_s, recv_s, send_t, recv_t) = refs
 
     sd, cols = x_ref.shape
     cb = modes * cols // nc
@@ -109,6 +114,8 @@
         return sorted(range(count), key=lambda d: -min(d, count - d))
 
     far_y = farthest(ys)
+    even = [dy for dy in far_y if dy % yls == 0]
+    odd = [dy for dy in far_y if dy % yls]
     q_steps = [(dc, dx) for dx in farthest(xs) for dc in (1, 0)][:-1]
 
     def z_at(m):
@@ -152,7 +159,7 @@
     loads = [
         pltpu.make_async_copy(src, dst, table_sem.at[n]) for n, (src, dst) in enumerate(zip(args_in, args))
     ]
-    for load in loads:
+    for load in loads[:5]:
         load.start()
 
     for n, dy in enumerate(far_y):
@@ -168,6 +175,9 @@
             return 0
 
         lax.fori_loop(0, zs if dyh else zs - 1, other, 0)
+
+    for load in loads[5:]:
+        load.start()
 
     width = min(cols, 256)
     row = lax.broadcasted_iota(jnp.int32, (width, width), 0)
@@ -189,20 +199,16 @@
             to_yl, to_x = c // nc // xs, c // nc % xs
             both = jnp.concatenate([part[r0 : r0 + zs] for part in pair_of], axis=0)
             s1[to_core * xs + to_x, to_yh * yls + to_yl] = both.astype(BF16)
-
-    pl.semaphore_wait(barrier, (ys * zs - 1) + (qs - 1) + (yhs * zs - 1))
-
-    def copy(device, src, dst, send, recv):
-        return pltpu.make_async_remote_copy(
-            src_ref=src, dst_ref=dst, send_sem=send, recv_sem=recv, device_id=device, device_id_type=MESH
-        )
-
-    some_chip, _ = chip_peer(q_steps[0])
-    for n, dy in enumerate(far_y):
-        for step in q_steps:
-            device, q_at = chip_peer(step)
-            copy(device, s1.at[q_at, y_at(dy)], r1.at[q_me, y_at(dy)], send1, recv1.at[n]).start()
-    r1[pl.ds(q_me, 1)] = s1[pl.ds(q_me, 1)]
+        for r0 in range(0, width, run):
+            for arr in range(2):
+                runs[arr, (c0 + r0) // run] = pair_of[arr][r0 : r0 + run].astype(BF16)
+    loads[5].wait()
+    for dy in odd:
+        there = y_at(dy)
+        first_run = lax.rem(there, yls) * xs * yhs + there // yls
+        piece = [runs[arr, first_run + to_x * yhs] for arr in range(2) for to_x in range(xs)]
+        piece = dot(moves[2], jnp.concatenate(piece, axis=0))
+        s3[pl.ds(there * zs, zs)] = piece.astype(BF16).reshape(zs, qs * 2, sd)
 
     for n in (2, 3, 4):
         loads[n].wait()
@@ -247,6 +253,13 @@
 
     lax.fori_loop(0, nblk, states, 0)
 
+    def copy(device, src, dst, send, recv):
+        return pltpu.make_async_remote_copy(
+            src_ref=src, dst_ref=dst, send_sem=send, recv_sem=recv, device_id=device, device_id_type=MESH
+        )
+
+    some_chip, _ = chip_peer(q_steps[0])
+    some_plane, _ = plane_peer(far_y[0], 0)
     def ctx_copy(peer, src, dst, send, recv):
         return copy({"ctx": peer}, src, dst, send, recv)
 
@@ -258,32 +271,42 @@
     def wait_ctx(own, everyone, send, recv, count=nc - 1):
         return ctx_copy(ctx_peer(0, 0), own.at[pl.ds(0, count)], everyone.at[pl.ds(0, count)], send, recv)
 
+    pl.semaphore_wait(barrier, (ys * zs - 1) + (qs - 1) + (yhs * zs - 1))
+
+    def to_chip(source, target, y, send, recv):
+        for step in q_steps:
+            device, q_at = chip_peer(step)
+            copy(device, source.at[q_at, y], target.at[q_me, y], send, recv).start()
+        target[pl.ds(q_me, 1), pl.ds(y, 1)] = source[pl.ds(q_me, 1), pl.ds(y, 1)]
+
+    def to_plane(source, target, dy, send, recv):
+        def onward(device, at):
+            copy(device, source.at[at], target.at[y_me * zs + z], send, recv).start()
+
+        each_plane(dy, onward)
+
+    def wait_chip(source, target, send, recv):
+        return copy(some_chip, source.at[pl.ds(0, qs - 1), 0], target.at[pl.ds(0, qs - 1), 0], send, recv)
+
+    def wait_plane(source, target, count, send, recv):
+        return copy(some_plane, source.at[pl.ds(0, count)], target.at[pl.ds(0, count)], send, recv)
+
+    for n, dy in enumerate(even):
+        to_chip(s1, r1, y_at(dy), send1, recv1.at[n])
+    for dy in odd:
+        to_plane(s3, r3, dy, send3, recv3.at[y_me])
     send_to_ctx(u_own, u_all, send_u, recv_u)
 
-    for n, dy in enumerate(far_y):
-        copy(some_chip, s1.at[pl.ds(0, qs - 1), 0], r1.at[pl.ds(0, qs - 1), 0], send1, recv1.at[n]).wait_recv()
-        if n == 0:
-            loads[5].wait()
+    for n, dy in enumerate(even):
+        wait_chip(s1, r1, send1, recv1.at[n]).wait_recv()
         block = r1[:, pl.ds(y_at(dy), 1)].reshape(qs * 2 * zs, sd)
-        s2[pl.ds(y_at(dy) * zs, zs)] = dot(gather[...], block).astype(BF16).reshape(zs, qs * 2, sd)
-
-        def onward(device, at):
-            copy(device, s2.at[at], r2.at[y_me * zs + z], send2, recv2.at[y_me]).start()
-
-        each_plane(dy, onward)
+        s2[pl.ds(y_at(dy) * zs, zs)] = dot(moves[0], block).astype(BF16).reshape(zs, qs * 2, sd)
+        to_plane(s2, r2, dy, send2, recv2.at[y_me])
     own = pl.ds(y_me * zs + z, 1)
     r2[own] = s2[own]
 
-    wait_ctx(u_own, u_all, send_u, recv_u).wait_recv()
-    decay = jnp.exp(-rate_rows[me] * float(sd))
-    state = jnp.zeros((1, cb), F32)
-    for p in range(nc - 1, -1, -1):
-        st_own[p] = state
-        state = u_all[p] + decay * state
-    send_to_ctx(st_own, st_all, send_s, recv_s)
-
+    loads[10].wait()
     loads[11].wait()
-    loads[12].wait()
     wide = min(cols, 256)
 
     def inside(blk, _):
@@ -302,44 +325,61 @@
 
     lax.fori_loop(0, cols // wide, inside, 0)
 
-    for n in (6, 7, 8, 9, 10):
+    wait_ctx(u_own, u_all, send_u, recv_u).wait_recv()
+    decay = jnp.exp(-rate_rows[me] * float(sd))
+    state = jnp.zeros((1, cb), F32)
+    for p in range(nc - 1, -1, -1):
+        st_own[p] = state
+        state = u_all[p] + decay * state
+    send_to_ctx(st_own, st_all, send_s, recv_s)
+
+    for n, dy in enumerate(reversed(odd)):
+        wait_plane(s3, r3, zs, send3, recv3.at[y_at(dy)]).wait_recv()
+        block = r3[pl.ds(y_at(dy) * zs, zs)].reshape(zs * qs * 2, sd)
+        s4[:, pl.ds(y_at(dy), 1)] = dot(moves[3], block).astype(BF16).reshape(qs, 1, 2 * zs, sd)
+        to_chip(s4, r4, y_at(dy), send4, recv4.at[n])
+
+    for n in (6, 7, 8, 9):
         loads[n].wait()
-    some_plane, _ = plane_peer(far_y[0], 0)
-    for dy in reversed(far_y):
-        count = zs if dy else zs - 1
-        copy(
-            some_plane, s2.at[pl.ds(0, count)], r2.at[pl.ds(0, count)], send2, recv2.at[y_at(dy)]
-        ).wait_recv()
+    turn_c, turn_s = twist[0], twist[1]
+
+    def transform(part_of_y):
+        total_re, total_im = 0.0, 0.0
+        for q in range(xs // 2):
+            for k in range(4):
+                at = (2 * q + k // 2) * 2 + k % 2
+                part = [blocks[a * yls + part_of_y, at] for a in range(yhs)]
+                freq = dot(first[...], jnp.concatenate(part + part, axis=0))
+                re, im = freq[:nc], freq[nc:]
+                high_re, low_re = split(re * turn_c + im * turn_s)
+                high_im, low_im = split(im * turn_c - re * turn_s)
+                to = pl.ds(((k % 2) * 2 + k // 2) * nc, nc)
+                for n, piece in enumerate((high_re, high_im, low_re, low_im, high_re, high_im)):
+                    left[q, to, n * sd : (n + 1) * sd] = piece
+            both = dot(left[q], second[...])
+            x_re, x_im = both[: 2 * nc, :sd], both[: 2 * nc, sd:]
+            g_re, g_im = both[2 * nc :, :sd], both[2 * nc :, sd:]
+            re = x_re * g_re + x_im * g_im
+            im = x_re * g_im - x_im * g_re
+            total_re = total_re + re[:nc] + re[nc:]
+            total_im = total_im + im[:nc] + im[nc:]
+        return total_re, total_im
+
+    for n, dy in enumerate(reversed(odd)):
+        wait_chip(s4, r4, send4, recv4.at[n]).wait_recv()
+        block = r4[:, pl.ds(y_at(dy), 1)].reshape(qs * 2 * zs, sd)
+        blocks[pl.ds(y_at(dy), 1)] = dot(moves[4], block).astype(BF16).reshape(1, xs * 2, run, sd)
+    for d in range(1, yls):
+        spec[:, :sd], spec[:, sd:] = transform(lax.rem(yl + d, yls))
+    for dy in reversed(even):
+        wait_plane(s2, r2, zs if dy else zs - 1, send2, recv2.at[y_at(dy)]).wait_recv()
         block = r2[pl.ds(y_at(dy) * zs, zs)].reshape(zs * qs * 2, sd)
-        blocks[pl.ds(y_at(dy), 1)] = dot(spread[...], block).astype(BF16).reshape(1, xs * 2, run, sd)
-    turn_c, turn_s = twist[0], twist[1]
-    spec[...] = jnp.zeros_like(spec)
-
-    def pair(q, _):
-        for k in range(4):
-            share = 2 * q + k // 2
-            at = lax.rem(share, xs) * 2 + k % 2
-            part = [blocks[a * yls + share // xs, at] for a in range(yhs)]
-            freq = dot(first[...], jnp.concatenate(part + part, axis=0))
-            re, im = freq[:nc], freq[nc:]
-            high_re, low_re = split(re * turn_c + im * turn_s)
-            high_im, low_im = split(im * turn_c - re * turn_s)
-            at = pl.ds(((k % 2) * 2 + k // 2) * nc, nc)
-            for n, piece in enumerate((high_re, high_im, low_re, low_im, high_re, high_im)):
-                left[at, n * sd : (n + 1) * sd] = piece
-        both = dot(left[...], second[...])
-        x_re, x_im = both[: 2 * nc, :sd], both[: 2 * nc, sd:]
-        g_re, g_im = both[2 * nc :, :sd], both[2 * nc :, sd:]
-        re = x_re * g_re + x_im * g_im
-        im = x_re * g_im - x_im * g_re
-        spec[:, :sd] += re[:nc] + re[nc:]
-        spec[:, sd:] += im[:nc] + im[nc:]
-        return 0
-
-    lax.fori_loop(0, nh // 2, pair, 0)
-
-    re_h, re_l = split(spec[:, :sd])
-    im_h, im_l = split(-spec[:, sd:])
+        blocks[pl.ds(y_at(dy), 1)] = dot(moves[1], block).astype(BF16).reshape(1, xs * 2, run, sd)
+    spec_re, spec_im = transform(yl)
+    spec_re, spec_im = spec_re + spec[:, :sd], spec_im + spec[:, sd:]
+
+    re_h, re_l = split(spec_re)
+    im_h, im_l = split(-spec_im)
     both = dot(jnp.concatenate([re_h, im_h, re_l, im_l, re_h, im_h], axis=1), second[...])
     re, im = both[:, :sd], -both[:, sd:]
     high, low = split(
@@ -379,9 +419,11 @@
     out_ref[...] = gathered
 
     leave.wait()
-    copy(some_chip, s1.at[pl.ds(0, qs - 1)], r1.at[pl.ds(0, qs - 1)], send1, recv1.at[0]).wait_send()
-    rest = pl.ds(0, ys * zs - 1)
-    copy(some_plane, s2.at[rest], r2.at[rest], send2, recv2.at[0]).wait_send()
+    for source, target, send in ((s1, r1, send1), (s4, r4, send4)):
+        some = (pl.ds(0, qs - 1), pl.ds(0, len(even)))
+        copy(some_chip, source.at[some], target.at[some], send, recv1.at[0]).wait_send()
+    wait_plane(s2, r2, len(even) * zs - 1, send2, recv2.at[0]).wait_send()
+    wait_plane(s3, r3, len(odd) * zs, send3, recv3.at[0]).wait_send()
     wait_ctx(u_own, u_all, send_u, recv_u).wait_send()
     wait_ctx(st_own, st_all, send_s, recv_s).wait_send()
     wait_ctx(t_own, t_all, send_t, recv_t).wait_send()
@@ -412,10 +454,15 @@
         out_specs=(pl.BlockSpec(memory_space=pltpu.HBM), vmem),
         scratch_shapes=[pltpu.VMEM(arg.shape, arg.dtype) for arg in args]
         + [
+            pltpu.VMEM((2, cols // (zs * cores), zs * cores, sd), BF16),
             pltpu.VMEM((qs, ys, 2 * zs, sd), BF16),
             pltpu.VMEM((qs, ys, 2 * zs, sd), BF16),
             pltpu.VMEM((ys * zs, qs * 2, sd), BF16),
             pltpu.VMEM((ys * zs, qs * 2, sd), BF16),
+            pltpu.VMEM((ys * zs, qs * 2, sd), BF16),
+            pltpu.VMEM((ys * zs, qs * 2, sd), BF16),
+            pltpu.VMEM((qs, ys, 2 * zs, sd), BF16),
+            pltpu.VMEM((qs, ys, 2 * zs, sd), BF16),
             pltpu.VMEM((nc, 1, cb), F32),
             pltpu.VMEM((nc, 1, cb), F32),
             pltpu.VMEM((nc, 1, cb), F32),
@@ -429,13 +476,15 @@
             pltpu.VMEM((modes, cols), F32),
             pltpu.VMEM((nc, 1, cb), F32),
             pltpu.VMEM((ys, xs * 2, zs * cores, sd), BF16),
-            pltpu.VMEM((4 * nc, 6 * sd), BF16),
+            pltpu.VMEM((xs // 2, 4 * nc, 6 * sd), BF16),
             pltpu.VMEM((nc, 2 * sd), F32),
             dma((len(args),)),
             dma((ys,)),
             dma((ys,)),
+            dma((ys,)),
+            dma((ys,)),
         ]
-        + [dma] * 9,
+        + [dma] * 11,
         compiler_params=pltpu.CompilerParams(
             collective_id=0, has_side_effects=True, vmem_limit_bytes=64 * 1024 * 1024
         ),

time: 55.7 us -> 54.8 us (0.984)
  Pallas kernels: 54.9 us -> 54 us
    pallas_call x1, Pallas kernels: 53.1 us -> 52.2 us  [body(): pl.pallas_call(functools.partial(kernel, nc, nh, modes), out_shape=(jax.S...]
where the time goes in v3:
time: 54.8 us; the launch traced here: 54.7 us
  Pallas kernels  54 us (99%)
  between operations  0.64 us (1%)
    pallas_call x1, Pallas kernels, body(): pl.pallas_call(functools.partial(kernel, nc, nh, modes), out_shape=(jax.S...  52.2 us
    pallas_call x1, Pallas kernels, body(): pl.pallas_call(finish, out_shape=(jax.ShapeDtypeStruct((sd, cols), F32),...  1.88 us

profile of v3, /device:TPU:1, one launch (start us, length us, event | category | flops | bytes accessed | tf_op | source)
XLA Modules:
  0.0 54.7 jit_solution(767188387894974035)
XLA Ops:
  0.6 52.2 %modal_backward.1 = (f32[256,512]{1,0:T(8,128)}, f32[64,256]{1,0:T(8,128)}) custom-call(bf16[256,512]{1,0:T(8,128)(2,1)} %refs_0_.1, bf16[256,512]{1,0:T(8,128)(2,1)} %refs_1_.1, f32[16,512]{1,0:T(8,128)} %refs_2_.1, f32[16,512]{1,0:T(8,128)} %refs_3_.1, f32[1,512]{1,0:T(1,128)} %bitcast.2, bf16[5,128,128]{2,1,0:T(8,128)(2,1)} %constant.14.clone.refs_5_, ...), custom_call_target="tpu_custom_call" | custom-call | tf_op jit(solution)/shard_map/modal_backward/pallas_call | solution.py:447
  52.8 1.9 %finish.1 = (f32[256,512]{1,0:T(8,128)}, f32[64,256]{1,0:T(8,128)}) custom-call(f32[256,512]{1,0:T(8,128)} %get-tuple-element.6.input_in, f32[64,256]{1,0:T(8,128)} %get-tuple-element.7.filter_in), custom_call_target="tpu_custom_call" | custom-call | tf_op jit(solution)/shard_map/finish/pallas_call | solution.py:493

commit v4 on v3

--- a/solution.py
+++ b/solution.py
@@ -202,6 +202,46 @@
         for r0 in range(0, width, run):
             for arr in range(2):
                 runs[arr, (c0 + r0) // run] = pair_of[arr][r0 : r0 + run].astype(BF16)
+    def copy(device, src, dst, send, recv):
+        return pltpu.make_async_remote_copy(
+            src_ref=src, dst_ref=dst, send_sem=send, recv_sem=recv, device_id=device, device_id_type=MESH
+        )
+
+    some_chip, _ = chip_peer(q_steps[0])
+    some_plane, _ = plane_peer(far_y[0], 0)
+    def ctx_copy(peer, src, dst, send, recv):
+        return copy({"ctx": peer}, src, dst, send, recv)
+
+    def send_to_ctx(own, everyone, send, recv):
+        for dyh in farthest(yhs):
+            each_ctx(dyh, lambda peer: ctx_copy(peer, own.at[peer], everyone.at[me], send, recv).start())
+        everyone[pl.ds(me, 1)] = own[pl.ds(me, 1)]
+
+    def wait_ctx(own, everyone, send, recv, count=nc - 1):
+        return ctx_copy(ctx_peer(0, 0), own.at[pl.ds(0, count)], everyone.at[pl.ds(0, count)], send, recv)
+
+    pl.semaphore_wait(barrier, (ys * zs - 1) + (qs - 1) + (yhs * zs - 1))
+
+    def to_chip(source, target, y, send, recv):
+        for step in q_steps:
+            device, q_at = chip_peer(step)
+            copy(device, source.at[q_at, y], target.at[q_me, y], send, recv).start()
+        target[pl.ds(q_me, 1), pl.ds(y, 1)] = source[pl.ds(q_me, 1), pl.ds(y, 1)]
+
+    def to_plane(source, target, dy, send, recv):
+        def onward(device, at):
+            copy(device, source.at[at], target.at[y_me * zs + z], send, recv).start()
+
+        each_plane(dy, onward)
+
+    def wait_chip(source, target, send, recv):
+        return copy(some_chip, source.at[pl.ds(0, qs - 1), 0], target.at[pl.ds(0, qs - 1), 0], send, recv)
+
+    def wait_plane(source, target, count, send, recv):
+        return copy(some_plane, source.at[pl.ds(0, count)], target.at[pl.ds(0, count)], send, recv)
+
+    for n, dy in enumerate(even):
+        to_chip(s1, r1, y_at(dy), send1, recv1.at[n])
     loads[5].wait()
     for dy in odd:
         there = y_at(dy)
@@ -209,6 +249,7 @@
         piece = [runs[arr, first_run + to_x * yhs] for arr in range(2) for to_x in range(xs)]
         piece = dot(moves[2], jnp.concatenate(piece, axis=0))
         s3[pl.ds(there * zs, zs)] = piece.astype(BF16).reshape(zs, qs * 2, sd)
+        to_plane(s3, r3, dy, send3, recv3.at[y_me])
 
     for n in (2, 3, 4):
         loads[n].wait()
@@ -253,48 +294,6 @@
 
     lax.fori_loop(0, nblk, states, 0)
 
-    def copy(device, src, dst, send, recv):
-        return pltpu.make_async_remote_copy(
-            src_ref=src, dst_ref=dst, send_sem=send, recv_sem=recv, device_id=device, device_id_type=MESH
-        )
-
-    some_chip, _ = chip_peer(q_steps[0])
-    some_plane, _ = plane_peer(far_y[0], 0)
-    def ctx_copy(peer, src, dst, send, recv):
-        return copy({"ctx": peer}, src, dst, send, recv)
-
-    def send_to_ctx(own, everyone, send, recv):
-        for dyh in farthest(yhs):
-            each_ctx(dyh, lambda peer: ctx_copy(peer, own.at[peer], everyone.at[me], send, recv).start())
-        everyone[pl.ds(me, 1)] = own[pl.ds(me, 1)]
-
-    def wait_ctx(own, everyone, send, recv, count=nc - 1):
-        return ctx_copy(ctx_peer(0, 0), own.at[pl.ds(0, count)], everyone.at[pl.ds(0, count)], send, recv)
-
-    pl.semaphore_wait(barrier, (ys * zs - 1) + (qs - 1) + (yhs * zs - 1))
-
-    def to_chip(source, target, y, send, recv):
-        for step in q_steps:
-            device, q_at = chip_peer(step)
-            copy(device, source.at[q_at, y], target.at[q_me, y], send, recv).start()
-        target[pl.ds(q_me, 1), pl.ds(y, 1)] = source[pl.ds(q_me, 1), pl.ds(y, 1)]
-
-    def to_plane(source, target, dy, send, recv):
-        def onward(device, at):
-            copy(device, source.at[at], target.at[y_me * zs + z], send, recv).start()
-
-        each_plane(dy, onward)
-
-    def wait_chip(source, target, send, recv):
-        return copy(some_chip, source.at[pl.ds(0, qs - 1), 0], target.at[pl.ds(0, qs - 1), 0], send, recv)
-
-    def wait_plane(source, target, count, send, recv):
-        return copy(some_plane, source.at[pl.ds(0, count)], target.at[pl.ds(0, count)], send, recv)
-
-    for n, dy in enumerate(even):
-        to_chip(s1, r1, y_at(dy), send1, recv1.at[n])
-    for dy in odd:
-        to_plane(s3, r3, dy, send3, recv3.at[y_me])
     send_to_ctx(u_own, u_all, send_u, recv_u)
 
     for n, dy in enumerate(even):
@@ -325,6 +324,12 @@
 
     lax.fori_loop(0, cols // wide, inside, 0)
 
+    for n, dy in enumerate(reversed(odd)):
+        wait_plane(s3, r3, zs, send3, recv3.at[y_at(dy)]).wait_recv()
+        block = r3[pl.ds(y_at(dy) * zs, zs)].reshape(zs * qs * 2, sd)
+        s4[:, pl.ds(y_at(dy), 1)] = dot(moves[3], block).astype(BF16).reshape(qs, 1, 2 * zs, sd)
+        to_chip(s4, r4, y_at(dy), send4, recv4.at[n])
+
     wait_ctx(u_own, u_all, send_u, recv_u).wait_recv()
     decay = jnp.exp(-rate_rows[me] * float(sd))
     state = jnp.zeros((1, cb), F32)
@@ -332,12 +337,6 @@
         st_own[p] = state
         state = u_all[p] + decay * state
     send_to_ctx(st_own, st_all, send_s, recv_s)
-
-    for n, dy in enumerate(reversed(odd)):
-        wait_plane(s3, r3, zs, send3, recv3.at[y_at(dy)]).wait_recv()
-        block = r3[pl.ds(y_at(dy) * zs, zs)].reshape(zs * qs * 2, sd)
-        s4[:, pl.ds(y_at(dy), 1)] = dot(moves[3], block).astype(BF16).reshape(qs, 1, 2 * zs, sd)
-        to_chip(s4, r4, y_at(dy), send4, recv4.at[n])
 
     for n in (6, 7, 8, 9):
         loads[n].wait()

time: 54.8 us -> 50.4 us (0.920)
  Pallas kernels: 54 us -> 49.6 us
    pallas_call x1, Pallas kernels: 52.2 us -> 47.7 us  [body(): pl.pallas_call(functools.partial(kernel, nc, nh, modes), out_shape=(jax.S...]
where the time goes in v4:
time: 50.4 us; the launch traced here: 50.3 us
  Pallas kernels  49.6 us (98%)
  between operations  0.64 us (1%)
    pallas_call x1, Pallas kernels, body(): pl.pallas_call(functools.partial(kernel, nc, nh, modes), out_shape=(jax.S...  47.7 us
    pallas_call x1, Pallas kernels, body(): pl.pallas_call(finish, out_shape=(jax.ShapeDtypeStruct((sd, cols), F32),...  1.88 us

profile of v4, /device:TPU:1, one launch (start us, length us, event | category | flops | bytes accessed | tf_op | source)
XLA Modules:
  0.0 50.3 jit_solution(10610543230536425855)
XLA Ops:
  0.6 47.7 %modal_backward.1 = (f32[256,512]{1,0:T(8,128)}, f32[64,256]{1,0:T(8,128)}) custom-call(bf16[256,512]{1,0:T(8,128)(2,1)} %refs_0_.1, bf16[256,512]{1,0:T(8,128)(2,1)} %refs_1_.1, f32[16,512]{1,0:T(8,128)} %refs_2_.1, f32[16,512]{1,0:T(8,128)} %refs_3_.1, f32[1,512]{1,0:T(1,128)} %bitcast.2, bf16[5,128,128]{2,1,0:T(8,128)(2,1)} %constant.14.clone.refs_5_, ...), custom_call_target="tpu_custom_call" | custom-call | tf_op jit(solution)/shard_map/modal_backward/pallas_call | solution.py:446
  48.4 1.9 %finish.1 = (f32[256,512]{1,0:T(8,128)}, f32[64,256]{1,0:T(8,128)}) custom-call(f32[256,512]{1,0:T(8,128)} %get-tuple-element.6.input_in, f32[64,256]{1,0:T(8,128)} %get-tuple-element.7.filter_in), custom_call_target="tpu_custom_call" | custom-call | tf_op jit(solution)/shard_map/finish/pallas_call | solution.py:492

commit v5 on v4

--- a/solution.py
+++ b/solution.py
@@ -202,6 +202,7 @@
         for r0 in range(0, width, run):
             for arr in range(2):
                 runs[arr, (c0 + r0) // run] = pair_of[arr][r0 : r0 + run].astype(BF16)
+
     def copy(device, src, dst, send, recv):
         return pltpu.make_async_remote_copy(
             src_ref=src, dst_ref=dst, send_sem=send, recv_sem=recv, device_id=device, device_id_type=MESH
@@ -209,6 +210,7 @@
 
     some_chip, _ = chip_peer(q_steps[0])
     some_plane, _ = plane_peer(far_y[0], 0)
+
     def ctx_copy(peer, src, dst, send, recv):
         return copy({"ctx": peer}, src, dst, send, recv)
 
@@ -249,7 +251,14 @@
         piece = [runs[arr, first_run + to_x * yhs] for arr in range(2) for to_x in range(xs)]
         piece = dot(moves[2], jnp.concatenate(piece, axis=0))
         s3[pl.ds(there * zs, zs)] = piece.astype(BF16).reshape(zs, qs * 2, sd)
-        to_plane(s3, r3, dy, send3, recv3.at[y_me])
+
+    def both_ways(m, _):
+        for dy in odd:
+            device, at = plane_peer(dy, m)
+            copy(device, s3.at[at], r3.at[y_me * zs + z], send3, recv3.at[y_me]).start()
+        return 0
+
+    lax.fori_loop(0, zs, both_ways, 0)
 
     for n in (2, 3, 4):
         loads[n].wait()
@@ -343,25 +352,24 @@
     turn_c, turn_s = twist[0], twist[1]
 
     def transform(part_of_y):
-        total_re, total_im = 0.0, 0.0
-        for q in range(xs // 2):
-            for k in range(4):
-                at = (2 * q + k // 2) * 2 + k % 2
-                part = [blocks[a * yls + part_of_y, at] for a in range(yhs)]
+        half = xs * nc
+        for share in range(xs):
+            for arr in range(2):
+                part = [blocks[a * yls + part_of_y, share * 2 + arr] for a in range(yhs)]
                 freq = dot(first[...], jnp.concatenate(part + part, axis=0))
                 re, im = freq[:nc], freq[nc:]
                 high_re, low_re = split(re * turn_c + im * turn_s)
                 high_im, low_im = split(im * turn_c - re * turn_s)
-                to = pl.ds(((k % 2) * 2 + k // 2) * nc, nc)
-                for n, piece in enumerate((high_re, high_im, low_re, low_im, high_re, high_im)):
-                    left[q, to, n * sd : (n + 1) * sd] = piece
-            both = dot(left[q], second[...])
-            x_re, x_im = both[: 2 * nc, :sd], both[: 2 * nc, sd:]
-            g_re, g_im = both[2 * nc :, :sd], both[2 * nc :, sd:]
-            re = x_re * g_re + x_im * g_im
-            im = x_re * g_im - x_im * g_re
-            total_re = total_re + re[:nc] + re[nc:]
-            total_im = total_im + im[:nc] + im[nc:]
+                to = pl.ds(arr * half + share * nc, nc)
+                for n, piece in enumerate((high_re, high_im, low_re, low_im)):
+                    left[to, n * sd : (n + 1) * sd] = piece
+        both = dot(left[...], second[: 4 * sd]) + dot(left[:, : 2 * sd], second[4 * sd :])
+        x_re, x_im = both[:half, :sd], both[:half, sd:]
+        g_re, g_im = both[half:, :sd], both[half:, sd:]
+        re = x_re * g_re + x_im * g_im
+        im = x_re * g_im - x_im * g_re
+        total_re = sum(re[n * nc : (n + 1) * nc] for n in range(xs))
+        total_im = sum(im[n * nc : (n + 1) * nc] for n in range(xs))
         return total_re, total_im
 
     for n, dy in enumerate(reversed(odd)):
@@ -475,7 +483,7 @@
             pltpu.VMEM((modes, cols), F32),
             pltpu.VMEM((nc, 1, cb), F32),
             pltpu.VMEM((ys, xs * 2, zs * cores, sd), BF16),
-            pltpu.VMEM((xs // 2, 4 * nc, 6 * sd), BF16),
+            pltpu.VMEM((2 * xs * nc, 4 * sd), BF16),
             pltpu.VMEM((nc, 2 * sd), F32),
             dma((len(args),)),
             dma((ys,)),

time: 50.4 us -> 49.2 us (0.976)
  Pallas kernels: 49.6 us -> 48.4 us
    pallas_call x1, Pallas kernels: 47.7 us -> 46.5 us  [body(): pl.pallas_call(functools.partial(kernel, nc, nh, modes), out_shape=(jax.S...]
where the time goes in v5:
time: 49.2 us; the launch traced here: 49 us
  Pallas kernels  48.4 us (98%)
  between operations  0.64 us (1%)
    pallas_call x1, Pallas kernels, body(): pl.pallas_call(functools.partial(kernel, nc, nh, modes), out_shape=(jax.S...  46.5 us
    pallas_call x1, Pallas kernels, body(): pl.pallas_call(finish, out_shape=(jax.ShapeDtypeStruct((sd, cols), F32),...  1.88 us

profile of v5, /device:TPU:1, one launch (start us, length us, event | category | flops | bytes accessed | tf_op | source)
XLA Modules:
  0.0 49.0 jit_solution(10218233163891012939)
XLA Ops:
  0.6 46.5 %modal_backward.1 = (f32[256,512]{1,0:T(8,128)}, f32[64,256]{1,0:T(8,128)}) custom-call(bf16[256,512]{1,0:T(8,128)(2,1)} %refs_0_.1, bf16[256,512]{1,0:T(8,128)(2,1)} %refs_1_.1, f32[16,512]{1,0:T(8,128)} %refs_2_.1, f32[16,512]{1,0:T(8,128)} %refs_3_.1, f32[1,512]{1,0:T(1,128)} %bitcast.2, bf16[5,128,128]{2,1,0:T(8,128)(2,1)} %constant.14.clone.refs_5_, ...), custom_call_target="tpu_custom_call" | custom-call | tf_op jit(solution)/shard_map/modal_backward/pallas_call | solution.py:454
  47.1 1.9 %finish.1 = (f32[256,512]{1,0:T(8,128)}, f32[64,256]{1,0:T(8,128)}) custom-call(f32[256,512]{1,0:T(8,128)} %get-tuple-element.6.input_in, f32[64,256]{1,0:T(8,128)} %get-tuple-element.7.filter_in), custom_call_target="tpu_custom_call" | custom-call | tf_op jit(solution)/shard_map/finish/pallas_call | solution.py:500

commit v6 on v5

--- a/solution.py
+++ b/solution.py
@@ -159,22 +159,23 @@
     loads = [
         pltpu.make_async_copy(src, dst, table_sem.at[n]) for n, (src, dst) in enumerate(zip(args_in, args))
     ]
-    for load in loads[:5]:
-        load.start()
-
-    for n, dy in enumerate(far_y):
-        each_plane(dy, greet)
-        if n == 2:
-            for step in q_steps:
-                greet(*chip_peer(step))
-
-    for dyh in farthest(yhs):
+    def greet_other_core(dyh):
         def other(m, _):
             device = (lax.rem(yh + dyh, yhs) * zs + z_at(m)) * cores + lax.rem(core + 1, cores)
             greet({"ctx": device}, 0)
             return 0
 
         lax.fori_loop(0, zs if dyh else zs - 1, other, 0)
+
+    for n, dy in enumerate(far_y):
+        each_plane(dy, greet)
+        if dy % yls == 0:
+            greet_other_core(dy // yls)
+        if n == 0:
+            for load in loads[:5]:
+                load.start()
+    for step in q_steps:
+        greet(*chip_peer(step))
 
     for load in loads[5:]:
         load.start()

time: 49.2 us -> 48.5 us (0.986)
  Pallas kernels: 48.4 us -> 47.7 us
    pallas_call x1, Pallas kernels: 46.5 us -> 45.9 us  [body(): pl.pallas_call(functools.partial(kernel, nc, nh, modes), out_shape=(jax.S...]
where the time goes in v6:
time: 48.5 us; the launch traced here: 48.4 us
  Pallas kernels  47.7 us (98%)
  between operations  0.64 us (1%)
    pallas_call x1, Pallas kernels, body(): pl.pallas_call(functools.partial(kernel, nc, nh, modes), out_shape=(jax.S...  45.9 us
    pallas_call x1, Pallas kernels, body(): pl.pallas_call(finish, out_shape=(jax.ShapeDtypeStruct((sd, cols), F32),...  1.88 us

profile of v6, /device:TPU:1, one launch (start us, length us, event | category | flops | bytes accessed | tf_op | source)
XLA Modules:
  0.0 48.4 jit_solution(16043819753602993952)
XLA Ops:
  0.6 45.9 %modal_backward.1 = (f32[256,512]{1,0:T(8,128)}, f32[64,256]{1,0:T(8,128)}) custom-call(bf16[256,512]{1,0:T(8,128)(2,1)} %refs_0_.1, bf16[256,512]{1,0:T(8,128)(2,1)} %refs_1_.1, f32[16,512]{1,0:T(8,128)} %refs_2_.1, f32[16,512]{1,0:T(8,128)} %refs_3_.1, f32[1,512]{1,0:T(1,128)} %bitcast.2, bf16[5,128,128]{2,1,0:T(8,128)(2,1)} %constant.14.clone.refs_5_, ...), custom_call_target="tpu_custom_call" | custom-call | tf_op jit(solution)/shard_map/modal_backward/pallas_call | solution.py:455
  46.5 1.9 %finish.1 = (f32[256,512]{1,0:T(8,128)}, f32[64,256]{1,0:T(8,128)}) custom-call(f32[256,512]{1,0:T(8,128)} %get-tuple-element.6.input_in, f32[64,256]{1,0:T(8,128)} %get-tuple-element.7.filter_in), custom_call_target="tpu_custom_call" | custom-call | tf_op jit(solution)/shard_map/finish/pallas_call | solution.py:501

commit v7 on v6

--- a/solution.py
+++ b/solution.py
@@ -437,9 +437,19 @@
     wait_ctx(t_own, t_all, send_t, recv_t).wait_send()
 
 
-def finish(input_in, filter_in, input_out, filter_out):
-    input_out[...] = input_in[...]
-    filter_out[...] = filter_in[...]
+def finish(input_in, filter_in, input_out, filter_out, input_mid, filter_mid, sems):
+    rows = input_in.shape[0] // 4
+    pieces = [pl.ds(n * rows, rows) for n in range(4)]
+    steps = [(input_in.at[p], input_mid.at[p], input_out.at[p]) for p in pieces] + [(filter_in, filter_mid, filter_out)]
+    loads = [pltpu.make_async_copy(a, b, sems.at[n]) for n, (a, b, _) in enumerate(steps)]
+    stores = [pltpu.make_async_copy(b, c, sems.at[len(steps) + n]) for n, (_, b, c) in enumerate(steps)]
+    for load in loads:
+        load.start()
+    for load, store in zip(loads, stores):
+        load.wait()
+        store.start()
+    for store in stores:
+        store.wait()
 
 
 def body(nc, nh, inputs, out_grad, decay_rate, residue, skip_gain):
@@ -501,8 +511,9 @@
     input_grad, filter_grad = pl.pallas_call(
         finish,
         out_shape=(jax.ShapeDtypeStruct((sd, cols), F32), jax.ShapeDtypeStruct((nc, sd), F32)),
-        in_specs=[vmem, vmem],
-        out_specs=(vmem, vmem),
+        in_specs=[pl.BlockSpec(memory_space=pltpu.HBM)] * 2,
+        out_specs=(pl.BlockSpec(memory_space=pltpu.HBM),) * 2,
+        scratch_shapes=[pltpu.VMEM((sd, cols), F32), pltpu.VMEM((nc, sd), F32), dma((10,))],
         compiler_params=pltpu.CompilerParams(vmem_limit_bytes=64 * 1024 * 1024),
         name="finish",
     )(input_grad, filter_grad)

time: 48.5 us -> 48.5 us (level)
  no operation moved by 1% of the time
where the time goes in v7:
time: 48.5 us; the launch traced here: 48.3 us
  Pallas kernels  47.7 us (98%)
  between operations  0.64 us (1%)
    pallas_call x1, Pallas kernels, body(): pl.pallas_call(functools.partial(kernel, nc, nh, modes), out_shape=(jax.S...  45.9 us
    pallas_call x1, Pallas kernels, body(): pl.pallas_call(finish, out_shape=(jax.ShapeDtypeStruct((sd, cols), F32),...  1.85 us

profile of v7, /device:TPU:1, one launch (start us, length us, event | category | flops | bytes accessed | tf_op | source)
XLA Modules:
  0.0 48.3 jit_solution(3944679571011674709)
XLA Ops:
  0.6 45.9 %modal_backward.1 = (f32[256,512]{1,0:T(8,128)}, f32[64,256]{1,0:T(8,128)}) custom-call(bf16[256,512]{1,0:T(8,128)(2,1)} %refs_0_.1, bf16[256,512]{1,0:T(8,128)(2,1)} %refs_1_.1, f32[16,512]{1,0:T(8,128)} %refs_2_.1, f32[16,512]{1,0:T(8,128)} %refs_3_.1, f32[1,512]{1,0:T(1,128)} %bitcast.2, bf16[5,128,128]{2,1,0:T(8,128)(2,1)} %constant.14.clone.refs_5_, ...), custom_call_target="tpu_custom_call" | custom-call | tf_op jit(solution)/shard_map/modal_backward/pallas_call | solution.py:465
  46.5 1.9 %finish.1 = (f32[256,512]{1,0:T(8,128)}, f32[64,256]{1,0:T(8,128)}) custom-call(f32[256,512]{1,0:T(8,128)} %get-tuple-element.6.input_in, f32[64,256]{1,0:T(8,128)} %get-tuple-element.7.filter_in), custom_call_target="tpu_custom_call" | custom-call | tf_op jit(solution)/shard_map/finish/pallas_call | solution.py:511
